TPU v7x, 512 devices: a whole 4x4x16 slice. The times are simulated.
512 devices in a mesh: tm: 32 (over z, y_lo), space: 16 (over x, y_hi, core).
Axes of the slice: x: 4, y: 4 (y_hi: 2, y_lo: 2; y = y_hi * 2 + y_lo), z: 16, core: 2. Of those that a mesh axis runs over, the one named last changes fastest.
Arguments:
- inner_x: bfloat16 [32, 64, 64, 1536], P('tm', 'space'), may hold values from -6 to 6
- inner_z: bfloat16 [32, 64, 64, 1536], P('tm', 'space'), may hold values from -6 to 6
- conv_weight: float32 [4, 1536], P(None, 'space'), may hold values from -3 to 3
- conv_bias: float32 [1536], P('space'), may hold values from -0.5 to 0.5
- proj_weight: bfloat16 [1536, 80], P('space'), may hold values from -0.15625 to 0.15625
- step_weight: bfloat16 [48, 1536], P(None, 'space'), may hold values from -0.875 to 0.875
- step_bias: float32 [1536], P('space'), may hold values from -6.91 to -2.25, as said below
- decay_log: float32 [16, 1536], P(None, 'space'), may hold values from -2 to 2.77
- skip_gain: float32 [1536], P('space'), may hold values from 0.5 to 1.5
- out_weight: bfloat16 [1536, 768], replicated, may hold values from -0.15625 to 0.15625
- order_table: int32 [32], replicated, may hold values from 0 to 31, each once
Outputs:
- mixed: bfloat16 [32, 64, 64, 768], P('tm', 'space')
Inputs may be any that keep to these rules, and one draw needn't show every extreme that they name: order_table names each of the 32 blocks of a frame exactly once. step_bias is the inverse softplus of step sizes between 0.001 and 0.1.
All inputs are finite; a program needn't handle non-finite values.
Results may differ from a plain program's by a relative error of at most 0.017.
Values may be sent and summed in bfloat16 or wider, within the bound.
A program may use at most 128 MiB of HBM per device.

v0:
```python
import jax
import jax.numpy as jnp
from jax import lax
from jax.sharding import PartitionSpec as P

NS = 16
DTR = 48
KC = 4
BLK = 128


def shifted(block, axis, distance):
    devices = range(lax.axis_size(axis))
    route = [(i - distance, i) for i in devices if i - distance in devices]
    return lax.ppermute(block, axis, route)


def entering_2(part, axis, combine, identity):
    place = lax.axis_index(axis)
    gathered = jax.tree.map(lambda a: lax.all_gather(a, axis), part)
    state = jax.tree.map(lambda a, e: jnp.zeros_like(a) + jnp.asarray(e, a.dtype), part, identity)

    def one(lap, state):
        return combine(
            state, jax.tree.map(lambda a: lax.dynamic_index_in_dim(a, lap, 0, False), gathered)
        )

    return lax.fori_loop(0, place, one, state)


def to_scan_order(values, order_table):
    frames, length, columns = values.shape
    blocks = values.reshape(frames, length // BLK, BLK, columns)
    return jnp.take(blocks, order_table, axis=1).reshape(frames, length, columns)


def to_raster_order(values, order_table):
    frames, length, columns = values.shape
    blocks = values.reshape(frames, length // BLK, BLK, columns)
    placed = jnp.zeros_like(blocks).at[:, order_table].set(blocks)
    return placed.reshape(frames, length, columns)


def prefix_states(decays, states):
    count = decays.shape[0]
    if count <= 8 or count % 8 != 0:
        run_dec = jnp.ones_like(decays[0])
        run_state = jnp.zeros_like(states[0])
        dec_list = []
        state_list = []
        for offset in range(count):
            dec_list.append(run_dec)
            state_list.append(run_state)
            run_state = decays[offset] * run_state + states[offset]
            run_dec = decays[offset] * run_dec
        return (jnp.stack(dec_list), jnp.stack(state_list), run_dec, run_state)
    grouped_dec = decays.reshape((count // 8, 8) + decays.shape[1:])
    grouped_state = states.reshape((count // 8, 8) + states.shape[1:])
    run_dec = jnp.ones_like(grouped_dec[:, 0])
    run_state = jnp.zeros_like(grouped_state[:, 0])
    dec_list = []
    state_list = []
    for offset in range(8):
        dec_list.append(run_dec)
        state_list.append(run_state)
        run_state = grouped_dec[:, offset] * run_state + grouped_state[:, offset]
        run_dec = grouped_dec[:, offset] * run_dec
    block_dec, block_state, total_dec, total_state = prefix_states(run_dec, run_state)
    part_dec = jnp.stack(dec_list, axis=1)
    part_state = jnp.stack(state_list, axis=1)
    excl_dec = part_dec * block_dec[:, None]
    excl_state = part_dec * block_state[:, None] + part_state
    return (
        excl_dec.reshape(decays.shape),
        excl_state.reshape(states.shape),
        total_dec,
        total_state,
    )


def combine(earlier, later):
    return (later[0] * earlier[0], later[0] * earlier[1] + later[1])


def shards(
    inner_x,
    inner_z,
    conv_weight,
    conv_bias,
    proj_weight,
    step_weight,
    step_bias,
    decay_log,
    skip_gain,
    out_weight,
    order_table,
):
    frames, rows, columns, channels = inner_x.shape
    local_rows = inner_x.reshape(frames, rows * columns, channels)
    gate_rows = inner_z.reshape(frames, rows * columns, channels)
    entered, gate_scan = (
        lax.all_to_all(local_rows, "space", split_axis=2, concat_axis=1, tiled=True),
        lax.all_to_all(gate_rows, "space", split_axis=2, concat_axis=1, tiled=True),
    )
    gate_scan = to_scan_order(gate_scan, order_table)
    entered = to_scan_order(entered, order_table)
    frame_len = entered.shape[1]
    width_band = entered.shape[2]
    seq_len = frames * frame_len
    sequence = entered.reshape(seq_len, width_band)
    tail_rows = shifted(sequence[seq_len - (KC - 1) :], "tm", 1)
    padded = jnp.concatenate([tail_rows, sequence], axis=0).astype(jnp.float32)
    filtered = conv_bias[None, :] + sum(
        (conv_weight[tap][None, :] * padded[tap : tap + seq_len] for tap in range(KC))
    )
    signal = jax.nn.silu(filtered).astype(jnp.bfloat16)
    partial_sums = jnp.dot(signal, proj_weight, preferred_element_type=jnp.float32)
    projected = lax.psum(partial_sums, "space")
    step_size = jax.nn.softplus(
        jnp.dot(
            projected[:, :DTR], step_weight.astype(jnp.float32), precision=lax.Precision.HIGHEST
        )
        + step_bias[None, :]
    )
    in_coeff = projected[:, DTR : DTR + NS]
    out_coeff = projected[:, DTR + NS :]
    rate = -jnp.exp(decay_log)
    signal_f = signal.astype(jnp.float32)
    nblocks = seq_len // 8
    step_blocks = step_size.reshape(nblocks, 8, width_band)
    local_sum = jnp.cumsum(step_blocks, axis=1)
    drive_blocks = (step_size * signal_f).reshape(nblocks, 8, width_band)
    in_blocks = in_coeff.reshape(nblocks, 8, NS)
    out_blocks = out_coeff.reshape(nblocks, 8, NS)

    def weighted_inputs(upto):
        total = None
        for source in range(upto + 1):
            reach = local_sum[:, upto] - local_sum[:, source]
            term = (
                jnp.exp(reach[:, None, :] * rate[None])
                * in_blocks[:, source, :, None]
                * drive_blocks[:, source, None, :]
            )
            total = term if total is None else total + term
        return total

    total_dec = jnp.exp(local_sum[:, 7, None, :] * rate[None])
    total_state = weighted_inputs(7)
    excl_dec, excl_state, device_dec, device_state = prefix_states(total_dec, total_state)
    carried = entering_2(
        (device_dec, device_state),
        "tm",
        combine,
        (jnp.ones_like(device_dec), jnp.zeros_like(device_state)),
    )
    incoming = carried[1]
    entering = excl_dec * incoming[None] + excl_state
    results = []
    for offset in range(8):
        entry_decay = jnp.exp(local_sum[:, offset, None, :] * rate[None])
        state_now = entry_decay * entering + weighted_inputs(offset)
        results.append(jnp.sum(out_blocks[:, offset, :, None] * state_now, axis=1))
    scanned = jnp.stack(results, axis=1).reshape(seq_len, width_band)
    scanned = (scanned + skip_gain[None, :] * signal_f).astype(jnp.bfloat16)
    gate_f = gate_scan.reshape(seq_len, width_band).astype(jnp.float32)
    outgoing = (scanned.astype(jnp.float32) * jax.nn.silu(gate_f)).astype(jnp.bfloat16)
    outgoing = to_raster_order(outgoing.reshape(frames, frame_len, width_band), order_table)
    returned = lax.all_to_all(outgoing, "space", split_axis=1, concat_axis=2, tiled=True)
    returned = returned.reshape(frames * rows * columns, channels)
    output = jnp.dot(returned, out_weight, preferred_element_type=jnp.float32).astype(jnp.bfloat16)
    return output.reshape(frames, rows, columns, out_weight.shape[1])


def solution(mesh):
    in_specs = (
        P("tm", "space", None, None),
        P("tm", "space", None, None),
        P(None, "space"),
        P("space"),
        P("space", None),
        P(None, "space"),
        P("space"),
        P(None, "space"),
        P("space"),
        P(),
        P(),
    )
    out_specs = P("tm", "space", None, None)
    return jax.shard_map(shards, mesh=mesh, in_specs=in_specs, out_specs=out_specs, check_vma=False)
```

profile of v0, /device:TPU:489, one launch (start us, length us, event | category | flops | bytes accessed | tf_op | source)
XLA Modules:
  0.0 780.4 jit_solution(13402367271437088591)
XLA Ops:
  6.5 4.9 copy.395
  12.0 9.2 %reduce.8 = bf16[1536,256]{1,0:T(8,128)(2,1)S(1)} reduce(bf16[1536,1,256]{2,1,0:T(2,128)(2,1)} %bitcast.345, bf16[]{:T(256)} %broadcast.290), dimensions={1}, to_apply=%bitcast.313.reduce_sub_computation | reduce | bytes 1572866
  22.3 6.7 all-to-all-start
  29.0 4.7 copy.498
  33.8 9.2 %reduce.9 = bf16[1536,256]{1,0:T(8,128)(2,1)S(1)} reduce(bf16[1536,1,256]{2,1,0:T(2,128)(2,1)} %bitcast.348, bf16[]{:T(256)} %broadcast.290), dimensions={1}, to_apply=%bitcast.311.reduce_sub_computation | reduce | bytes 1572866
  44.0 7.2 all-to-all-start.1
  51.9 5.2 reshape.516
  61.7 3.8 all-to-all-done.1
  65.5 5.2 reshape.514
  75.7 2.3 copy.563
  81.4 2.5 bitcast_select_fusion.1
  84.7 13.1 %collective-permute-start = (bf16[3,96]{0,1:T(8,128)(2,1)S(1)}, bf16[3,96]{0,1:T(8,128)(2,1)S(1)}, u32[]{:S(2)}, u32[]{:S(2)}) collective-permute-start(bf16[3,96]{0,1:T(8,128)(2,1)S(1)} %slice.557), channel_id=1, source_target_pairs={{0,16},{16,32},{32,48},{48,64},{64,80},{80,96},{96,112},{112,128},... | collective-permute-start | bytes 1736 | tf_op jit(solution)/shard_map/ppermute | solution.py:15
  105.6 3.5 copy.501
  109.1 147.2 %all-reduce.2.cloned.1.call-done = f32[4096,80]{0,1:T(8,128)} async-done(((f32[4096,80]{0,1:T(8,128)}), f32[4096,80]{0,1:T(8,128)}) %all-reduce.2.cloned.1.call-update) | async-done | bytes 1310736 | tf_op jit(solution)/shard_map/psum | solution.py:118
  256.3 4.5 convert_multiply_fusion.1
  260.8 2.8 copy.401
  263.7 68.3 %reduce_window_sum.11 = f32[512,8,96]{2,1,0:T(8,128)} reduce-window(f32[512,8,96]{2,1,0:T(8,128)} %bitcast.339, f32[]{:T(128)} %constant.33.clone.1), window={size=1x8x1 pad=0_0x7_0x0_0}, to_apply=%region_1.3 | reduce-window | flops 2752512 | bytes 3145732 | tf_op jit(solution)/shard_map/jit(cumsum)/reduce_window_sum | solution.py:131
  332.0 8.2 %fusion.32 = (f32[512,1,96]{2,1,0:T(1,128)}, f32[512,1,96]{2,1,0:T(1,128)}, f32[512,1,96]{2,1,0:T(1,128)S(1)}, f32[512,1,96]{2,1,0:T(1,128)S(1)}, f32[512,1,96]{...) fusion(f32[512,8,96]{2,1,0:T(8,128)} %reduce_window_sum.11), kind=kLoop, calls=%fused_computation.223 | loop fusion | flops 540672 | bytes 3538944 | tf_op jit(solution)/shard_map/slice | solution.py:139
  340.2 3.9 slice_subtract_fusion.5
  344.1 3.3 slice_subtract_fusion.6
  347.4 4.5 slice_subtract_fusion.4
  357.9 2.8 copy.416
  360.7 8.6 %fusion.34 = (f32[512,1,96]{2,1,0:T(1,128)S(1)}, f32[512,1,96]{2,1,0:T(1,128)S(1)}, f32[512,1,96]{2,1,0:T(1,128)S(1)}, f32[512,1,96]{2,1,0:T(1,128)S(1)}, f32[51...) fusion(f32[512,8,96]{2,1,0:T(8,128)} %bitcast.338), kind=kLoop, calls=%fused_computation.225 | loop fusion | bytes 3145728 | tf_op jit(solution)/shard_map/slice | solution.py:143
  374.5 2.9 copy.414
  377.4 8.6 %fusion.33 = (f32[512,1,16]{2,1,0:T(1,128)S(1)}, f32[512,1,16]{2,1,0:T(1,128)S(1)}, f32[512,1,16]{2,1,0:T(1,128)S(1)}, f32[512,1,16]{2,1,0:T(1,128)S(1)}, f32[51...) fusion(f32[512,8,16]{2,1,0:T(8,128)} %bitcast.341), kind=kLoop, calls=%fused_computation.224 | loop fusion | bytes 524288 | tf_op jit(solution)/shard_map/slice | solution.py:142
  388.7 9.5 %multiply_add_fusion = f32[64,8,16,96]{3,2,0,1:T(8,128)S(1)} fusion(f32[64,8,96]{2,0,1:T(8,128)S(1)} %copy-done.52, f32[64,8,16]{2,0,1:T(8,128)S(1)} %copy.437, f32[64,8,96]{2,0,1:T(8,128)S(1)} %copy-done.48, f32[64,8,96]{2,0,1:T(8,128)S(1)} %copy-done.28, f32[64,8,16]{2,0,1:T(8,128)S(1)} %copy.434, f32[64,8,96]{2,0,1:T(8,128)S(1)} %copy-done.50, ...), kind=kLoop, calls=%fused_computation.16 | loop fusion | flops 24379392 | bytes 6559744 | tf_op jit(solution)/shard_map/add | solution.py:145
  398.3 2.3 fusion.29
  408.0 50.7 %all_gather.8 = f32[32,16,96]{2,1,0:T(8,128)} all-gather(f32[1,16,96]{2,1,0:T(8,128)S(1)} %get-tuple-element.194), channel_id=1, replica_groups=mesh['tm'=32,'space'=16] {'tm'}, dimensions={0}, use_global_device_ids=true | all-gather | bytes 202752 | tf_op jit(solution)/shard_map/all_gather | solution.py:20
  458.7 52.8 %all_gather.9 = f32[32,16,96]{2,1,0:T(8,128)} all-gather(f32[1,16,96]{2,1,0:T(8,128)S(1)} %get-tuple-element.71), channel_id=1, replica_groups=mesh['tm'=32,'space'=16] {'tm'}, dimensions={0}, use_global_device_ids=true | all-gather | bytes 202752 | tf_op jit(solution)/shard_map/all_gather | solution.py:20
  511.5 22.3 %while.12 = (s32[]{:T(128)}, f32[16,96]{1,0:T(8,128)S(1)}, s32[]{:T(128)}, f32[32,16,96]{2,1,0:T(8,128)}, f32[32,16,96]{2,1,0:T(8,128)}, /*index=5*/s32[]{:T(128)}, s32[]{:T(128)}, s32[]{:T(128)}) while((s32[]{:T(128)}, f32[16,96]{1,0:T(8,128)S(1)}, s32[]{:T(128)}, f32[32,16,96]{2,1,0:T(8,128)}, f32[32,16,96]{2,1,0:T(8,128)}, ...), condition=%wide.region_3.5_spmd, body=%wide.region_2.4_spmd.sunk | while | flops 3077 | bytes 24699 | solution.py:28
  553.1 2.9 copy.399
  556.0 9.4 %fusion.31 = (f32[512,1,16]{2,1,0:T(1,128)S(1)}, f32[512,1,16]{2,1,0:T(1,128)S(1)}, f32[512,1,16]{2,1,0:T(1,128)S(1)}, f32[512,1,16]{2,1,0:T(1,128)S(1)}, f32[51...) fusion(f32[512,8,16]{2,1,0:T(8,128)} %bitcast.342), kind=kLoop, calls=%fused_computation.222 | loop fusion | bytes 524288 | tf_op jit(solution)/shard_map/slice | solution.py:163
  597.9 18.9 %multiply_reduce_fusion = (f32[64,8,96]{2,0,1:T(8,128)}, f32[64,8,16,96]{3,2,0,1:T(8,128)}) fusion(f32[64,8,16]{2,0,1:T(8,128)} %copy.494, f32[16,96]{1,0:T(8,128)S(1)} %exponential_negate_fusion, f32[64,8,96]{2,0,1:T(8,128)S(1)} %copy-done.15, f32[64,8,16,96]{3,2,0,1:T(8,128)S(1)} %copy-done.7, f32[64,8,16,96]{3,2,0,1:T(8,128)S(1)} %copy-done.8, ...), kind=kLoop, calls=%fused_computation.7 | loop fusion | flops 32194560 | bytes 14069760 | tf_op jit(solution)/shard_map/reduce_sum | solution.py:163
  616.9 10.5 %multiply_reduce_fusion.4 = (f32[64,8,96]{2,0,1:T(8,128)S(1)}, f32[64,8,96]{2,0,1:T(8,128)S(1)}) fusion(f32[64,8,16,96]{3,2,0,1:T(8,128)} %get-tuple-element.66, f32[64,8,96]{2,0,1:T(8,128)} %copy.465, f32[64,8,96]{2,0,1:T(8,128)} %copy.464, f32[64,8,96]{2,0,1:T(8,128)} %copy.463, f32[64,8,96]{2,0,1:T(8,128)} %copy.462, f32[64,8,96]{2,0,1:T(8,128)} %copy.461, ...), kind=kLoop, calls=%fused_computation.11 | loop fusion | flops 21921792 | bytes 5904384 | tf_op jit(solution)/shard_map/reduce_sum | solution.py:163
  627.9 8.4 %multiply_reduce_fusion.5 = (f32[64,8,96]{2,0,1:T(8,128)S(1)}, f32[64,8,96]{2,0,1:T(8,128)S(1)}) fusion(f32[64,8,16,96]{3,2,0,1:T(8,128)S(1)} %copy-done.13, f32[64,8,96]{2,0,1:T(8,128)S(1)} %copy-done.121, f32[64,8,96]{2,0,1:T(8,128)S(1)} %copy-done.120, f32[64,8,96]{2,0,1:T(8,128)S(1)} %copy-done.119, f32[64,8,96]{2,0,1:T(8,128)S(1)} %copy-done.123, ...), kind=kLoop, calls=%fused_computation.12 | loop fusion | flops 21921792 | bytes 5675008 | tf_op jit(solution)/shard_map/reduce_sum | solution.py:163
  637.0 8.0 %multiply_reduce_fusion.3 = f32[64,8,96]{2,0,1:T(8,128)S(1)} fusion(f32[64,8,16,96]{3,2,0,1:T(8,128)S(1)} %copy-done.13, f32[64,8,96]{2,0,1:T(8,128)S(1)} %copy-done.111, f32[64,8,96]{2,0,1:T(8,128)S(1)} %copy-done.115, f32[64,8,96]{2,0,1:T(8,128)S(1)} %copy-done.114, f32[64,8,96]{2,0,1:T(8,128)S(1)} %copy-done.113, f32[64,8,96]{2,0,1:T(8,128)S(1)} %copy-done.112, ...), kind=kLoop, calls=%fused_computation.10 | loop fusion | flops 18825216 | bytes 5707776 | tf_op jit(solution)/shard_map/reduce_sum | solution.py:163
  645.4 9.1 %multiply_reduce_fusion.2 = f32[64,8,96]{2,0,1:T(8,128)S(1)} fusion(f32[64,8,16,96]{3,2,0,1:T(8,128)S(1)} %copy-done.13, f32[64,8,96]{2,0,1:T(8,128)S(1)} %copy-done.108, f32[64,8,96]{2,0,1:T(8,128)S(1)} %copy-done.107, f32[64,8,96]{2,0,1:T(8,128)S(1)} %copy-done.106, f32[64,8,96]{2,0,1:T(8,128)S(1)} %copy-done.105, f32[64,8,96]{2,0,1:T(8,128)S(1)} %copy-done.104, ...), kind=kLoop, calls=%fused_computation.9 | loop fusion | flops 21970944 | bytes 6133760 | tf_op jit(solution)/shard_map/reduce_sum | solution.py:163
  654.8 10.2 %multiply_reduce_fusion.1 = f32[64,8,96]{2,0,1:T(8,128)S(1)} fusion(f32[64,8,16,96]{3,2,0,1:T(8,128)S(1)} %copy-done.13, f32[64,8,96]{2,0,1:T(8,128)S(1)} %copy-done.99, f32[64,8,96]{2,0,1:T(8,128)S(1)} %copy-done.98, f32[64,8,96]{2,0,1:T(8,128)S(1)} %copy-done.97, f32[64,8,96]{2,0,1:T(8,128)S(1)} %copy-done.96, f32[64,8,96]{2,0,1:T(8,128)S(1)} %copy-done.95, ...), kind=kLoop, calls=%fused_computation.8 | loop fusion | flops 25116672 | bytes 6559744 | tf_op jit(solution)/shard_map/reduce_sum | solution.py:163
  665.5 2.5 copy.561
  668.0 2.9 copy.497
  670.9 6.7 copy_bitcast_fusion.2
  677.8 3.5 scatter_fusion
  682.6 6.9 reshape.512
  689.5 23.7 %reduce.10 = bf16[4096,96]{1,0:T(8,128)(2,1)S(1)} reduce(bf16[4096,1,96]{2,1,0:T(2,128)(2,1)} %bitcast.343, bf16[]{:T(256)} %broadcast.290), dimensions={1}, to_apply=%bitcast.315.reduce_sub_computation | reduce | bytes 1572866
  713.2 2.5 reshape.517
  715.7 47.0 %all_to_all.45 = bf16[16,2,12288]{2,1,0:T(2,128)(2,1)S(1)} all-to-all(bf16[16,2,12288]{2,1,0:T(2,128)(2,1)} %reshape.517), channel_id=1, replica_groups=mesh['tm'=32,'space'=16] {'space'}, dimensions={0} | all-to-all | bytes 1572864 | tf_op jit(solution)/shard_map/all_to_all | solution.py:169
  762.7 3.7 reshape.518
  766.4 4.6 copy.505
  (484 shorter events, 124.6 us)
Async XLA Ops:
  6.5 765.0 %copy-start = (bf16[1536,768]{1,0:T(8,128)(2,1)S(1)}, bf16[1536,768]{1,0:T(8,128)(2,1)}, u32[]{:S(2)}) copy-start(bf16[1536,768]{1,0:T(8,128)(2,1)} %param.24) | copy-start | bytes 7077892
  22.3 21.7 %all-to-all-start = ((bf16[16,2,12288]{2,1,0:T(2,128)(2,1)}), bf16[16,2,12288]{2,1,0:T(2,128)(2,1)}, u32[]{:S(2)}, u32[]{:S(2)}) async-start(bf16[16,2,12288]{2,1,0:T(2,128)(2,1)} %reshape.515), calls=%async_computation | async-start | bytes 1572864 | tf_op jit(solution)/shard_map/all_to_all | solution.py:102
  29.0 22.3 %copy-start.147 = (s32[32]{0:T(128)S(1)}, s32[32]{0:T(128)}, u32[]{:S(2)}) copy-start(s32[32]{0:T(128)} %param.25) | copy-start | bytes 388
  44.0 21.5 %all-to-all-start.1 = ((bf16[16,2,12288]{2,1,0:T(2,128)(2,1)}), bf16[16,2,12288]{2,1,0:T(2,128)(2,1)}, u32[]{:S(2)}, u32[]{:S(2)}) async-start(bf16[16,2,12288]{2,1,0:T(2,128)(2,1)} %reshape.513), calls=%async_computation.1 | async-start | bytes 1572864 | tf_op jit(solution)/shard_map/all_to_all | solution.py:103
  51.3 205.1 %all-reduce.2.cloned.1.call-start = ((), (), s32[]{:S(2)}) async-start(), calls=%async_computation.3 | async-start | bytes 2621440 | tf_op jit(solution)/shard_map/psum | solution.py:118
  79.6 18.1 %copy-start.142 = (f32[4,96]{1,0:T(4,128)S(1)}, f32[4,96]{1,0:T(4,128)}, u32[]{:S(2)}) copy-start(f32[4,96]{1,0:T(4,128)} %param.17) | copy-start | bytes 4612
  81.4 17.8 %copy-start.140 = (f32[96]{0:T(128)S(1)}, f32[96]{0:T(128)}, u32[]{:S(2)}) copy-start(f32[96]{0:T(128)} %param.18) | copy-start | bytes 1156
  84.7 13.1 %collective-permute-start = (bf16[3,96]{0,1:T(8,128)(2,1)S(1)}, bf16[3,96]{0,1:T(8,128)(2,1)S(1)}, u32[]{:S(2)}, u32[]{:S(2)}) collective-permute-start(bf16[3,96]{0,1:T(8,128)(2,1)S(1)} %slice.557), channel_id=1, source_target_pairs={{0,16},{16,32},{32,48},{48,64},{64,80},{80,96},{96,112},{112,128},... | collective-permute-start | bytes 1736 | tf_op jit(solution)/shard_map/ppermute | solution.py:15
  100.7 155.6 %copy-start.130 = (bf16[48,96]{1,0:T(8,128)(2,1)S(1)}, bf16[48,96]{1,0:T(8,128)(2,1)}, u32[]{:S(2)}) copy-start(bf16[48,96]{1,0:T(8,128)(2,1)} %param.20) | copy-start | bytes 27652
  100.7 155.6 %copy-start.145 = (f32[96]{0:T(128)S(1)}, f32[96]{0:T(128)}, u32[]{:S(2)}) copy-start(f32[96]{0:T(128)} %param.21) | copy-start | bytes 1156
  369.3 18.0 %copy-start.16 = (f32[64,8,96]{2,0,1:T(8,128)}, f32[64,8,96]{2,0,1:T(8,128)S(1)}, u32[]{:S(2)}) copy-start(f32[64,8,96]{2,0,1:T(8,128)S(1)} %copy.417) | copy-start | bytes 589828
  369.4 17.9 %copy-start.18 = (f32[64,8,96]{2,0,1:T(8,128)}, f32[64,8,96]{2,0,1:T(8,128)S(1)}, u32[]{:S(2)}) copy-start(f32[64,8,96]{2,0,1:T(8,128)S(1)} %copy.420) | copy-start | bytes 589828
  369.5 17.8 %copy-start.20 = (f32[64,8,96]{2,0,1:T(8,128)}, f32[64,8,96]{2,0,1:T(8,128)S(1)}, u32[]{:S(2)}) copy-start(f32[64,8,96]{2,0,1:T(8,128)S(1)} %copy.423) | copy-start | bytes 589828
  369.5 17.8 %copy-start.22 = (f32[64,8,96]{2,0,1:T(8,128)}, f32[64,8,96]{2,0,1:T(8,128)S(1)}, u32[]{:S(2)}) copy-start(f32[64,8,96]{2,0,1:T(8,128)S(1)} %copy.426) | copy-start | bytes 589828
  386.1 12.1 %copy-start.32 = (f32[64,8,16]{2,0,1:T(8,128)}, f32[64,8,16]{2,0,1:T(8,128)S(1)}, u32[]{:S(2)}) copy-start(f32[64,8,16]{2,0,1:T(8,128)S(1)} %copy.419) | copy-start | bytes 98308
  388.7 15.0 %copy-start.2 = (f32[64,8,16,96]{3,2,0,1:T(8,128)}, f32[64,8,16,96]{3,2,0,1:T(8,128)S(1)}, u32[]{:S(2)}) copy-start(f32[64,8,16,96]{3,2,0,1:T(8,128)S(1)} %multiply_exponential_fusion) | copy-start | bytes 9437188
  408.0 50.7 %copy-start.127 = (f32[8,16,96]{2,1,0:T(8,128)}, f32[8,16,96]{2,1,0:T(8,128)S(1)}, u32[]{:S(2)}) copy-start(f32[8,16,96]{2,1,0:T(8,128)S(1)} %get-tuple-element.193) | copy-start | bytes 147460
  533.9 13.5 %copy-start.128 = (f32[8,16,96]{2,1,0:T(8,128)S(1)}, f32[8,16,96]{2,1,0:T(8,128)}, u32[]{:S(2)}) copy-start(f32[8,16,96]{2,1,0:T(8,128)} %copy-done.127) | copy-start | bytes 147460
  555.9 12.5 %copy-start.88 = (f32[512,1,96]{2,1,0:T(1,128)S(1)}, f32[512,1,96]{2,1,0:T(1,128)}, u32[]{:S(2)}) copy-start(f32[512,1,96]{2,1,0:T(1,128)} %get-tuple-element.160) | copy-start | bytes 589828
  556.0 13.2 %copy-start.87 = (f32[512,1,96]{2,1,0:T(1,128)S(1)}, f32[512,1,96]{2,1,0:T(1,128)}, u32[]{:S(2)}) copy-start(f32[512,1,96]{2,1,0:T(1,128)} %get-tuple-element.161) | copy-start | bytes 589828
  556.0 13.9 %copy-start.86 = (f32[512,1,96]{2,1,0:T(1,128)S(1)}, f32[512,1,96]{2,1,0:T(1,128)}, u32[]{:S(2)}) copy-start(f32[512,1,96]{2,1,0:T(1,128)} %get-tuple-element.162) | copy-start | bytes 589828
  556.0 14.7 %copy-start.80 = (f32[512,1,96]{2,1,0:T(1,128)S(1)}, f32[512,1,96]{2,1,0:T(1,128)}, u32[]{:S(2)}) copy-start(f32[512,1,96]{2,1,0:T(1,128)} %get-tuple-element.158) | copy-start | bytes 589828
  556.0 15.4 %copy-start.83 = (f32[512,1,96]{2,1,0:T(1,128)S(1)}, f32[512,1,96]{2,1,0:T(1,128)}, u32[]{:S(2)}) copy-start(f32[512,1,96]{2,1,0:T(1,128)} %get-tuple-element.138) | copy-start | bytes 589828
  556.0 16.9 %copy-start.85 = (f32[512,1,96]{2,1,0:T(1,128)S(1)}, f32[512,1,96]{2,1,0:T(1,128)}, u32[]{:S(2)}) copy-start(f32[512,1,96]{2,1,0:T(1,128)} %get-tuple-element.163) | copy-start | bytes 589828
  556.0 17.7 %copy-start.79 = (f32[512,1,96]{2,1,0:T(1,128)S(1)}, f32[512,1,96]{2,1,0:T(1,128)}, u32[]{:S(2)}) copy-start(f32[512,1,96]{2,1,0:T(1,128)} %get-tuple-element.151) | copy-start | bytes 589828
  566.9 12.1 %copy-start.82 = (f32[512,1,96]{2,1,0:T(1,128)S(1)}, f32[512,1,96]{2,1,0:T(1,128)}, u32[]{:S(2)}) copy-start(f32[512,1,96]{2,1,0:T(1,128)} %get-tuple-element.164) | copy-start | bytes 589828
  570.7 12.1 %copy-start.69 = (f32[512,1,96]{2,1,0:T(1,128)S(1)}, f32[512,1,96]{2,1,0:T(1,128)}, u32[]{:S(2)}) copy-start(f32[512,1,96]{2,1,0:T(1,128)} %get-tuple-element.147) | copy-start | bytes 589828
  572.2 12.1 %copy-start.64 = (f32[512,1,96]{2,1,0:T(1,128)S(1)}, f32[512,1,96]{2,1,0:T(1,128)}, u32[]{:S(2)}) copy-start(f32[512,1,96]{2,1,0:T(1,128)} %get-tuple-element.131) | copy-start | bytes 589828
  573.7 12.1 %copy-start.60 = (f32[512,1,96]{2,1,0:T(1,128)S(1)}, f32[512,1,96]{2,1,0:T(1,128)}, u32[]{:S(2)}) copy-start(f32[512,1,96]{2,1,0:T(1,128)} %get-tuple-element.134) | copy-start | bytes 589828
  574.4 12.1 %copy-start.58 = (f32[512,1,96]{2,1,0:T(1,128)S(1)}, f32[512,1,96]{2,1,0:T(1,128)}, u32[]{:S(2)}) copy-start(f32[512,1,96]{2,1,0:T(1,128)} %get-tuple-element.135) | copy-start | bytes 589828
  575.2 12.1 %copy-start.56 = (f32[512,1,96]{2,1,0:T(1,128)S(1)}, f32[512,1,96]{2,1,0:T(1,128)}, u32[]{:S(2)}) copy-start(f32[512,1,96]{2,1,0:T(1,128)} %get-tuple-element.136) | copy-start | bytes 589828
  575.9 12.1 %copy-start.68 = (f32[512,1,96]{2,1,0:T(1,128)S(1)}, f32[512,1,96]{2,1,0:T(1,128)}, u32[]{:S(2)}) copy-start(f32[512,1,96]{2,1,0:T(1,128)} %get-tuple-element.167) | copy-start | bytes 589828
  576.7 12.1 %copy-start.67 = (f32[512,1,96]{2,1,0:T(1,128)S(1)}, f32[512,1,96]{2,1,0:T(1,128)}, u32[]{:S(2)}) copy-start(f32[512,1,96]{2,1,0:T(1,128)} %get-tuple-element.166) | copy-start | bytes 589828
  577.5 12.1 %copy-start.92 = (f32[512,1,16]{2,1,0:T(1,128)S(1)}, f32[512,1,16]{2,1,0:T(1,128)}, u32[]{:S(2)}) copy-start(f32[512,1,16]{2,1,0:T(1,128)} %get-tuple-element.124) | copy-start | bytes 98308
  578.2 12.1 %copy-start.91 = (f32[512,1,16]{2,1,0:T(1,128)S(1)}, f32[512,1,16]{2,1,0:T(1,128)}, u32[]{:S(2)}) copy-start(f32[512,1,16]{2,1,0:T(1,128)} %get-tuple-element.123) | copy-start | bytes 98308
  579.0 12.1 %copy-start.55 = (f32[512,1,96]{2,1,0:T(1,128)S(1)}, f32[512,1,96]{2,1,0:T(1,128)}, u32[]{:S(2)}) copy-start(f32[512,1,96]{2,1,0:T(1,128)} %get-tuple-element.127) | copy-start | bytes 589828
  579.7 12.1 %copy-start.66 = (f32[512,1,96]{2,1,0:T(1,128)S(1)}, f32[512,1,96]{2,1,0:T(1,128)}, u32[]{:S(2)}) copy-start(f32[512,1,96]{2,1,0:T(1,128)} %get-tuple-element.169) | copy-start | bytes 589828
  580.5 12.1 %copy-start.65 = (f32[512,1,96]{2,1,0:T(1,128)S(1)}, f32[512,1,96]{2,1,0:T(1,128)}, u32[]{:S(2)}) copy-start(f32[512,1,96]{2,1,0:T(1,128)} %get-tuple-element.165) | copy-start | bytes 589828
  581.2 12.1 %copy-start.63 = (f32[512,1,96]{2,1,0:T(1,128)S(1)}, f32[512,1,96]{2,1,0:T(1,128)}, u32[]{:S(2)}) copy-start(f32[512,1,96]{2,1,0:T(1,128)} %get-tuple-element.139) | copy-start | bytes 589828
  582.0 12.1 %copy-start.61 = (f32[512,1,96]{2,1,0:T(1,128)S(1)}, f32[512,1,96]{2,1,0:T(1,128)}, u32[]{:S(2)}) copy-start(f32[512,1,96]{2,1,0:T(1,128)} %get-tuple-element.140) | copy-start | bytes 589828
  582.7 12.1 %copy-start.59 = (f32[512,1,96]{2,1,0:T(1,128)S(1)}, f32[512,1,96]{2,1,0:T(1,128)}, u32[]{:S(2)}) copy-start(f32[512,1,96]{2,1,0:T(1,128)} %get-tuple-element.141) | copy-start | bytes 589828
  583.5 12.1 %copy-start.57 = (f32[512,1,96]{2,1,0:T(1,128)S(1)}, f32[512,1,96]{2,1,0:T(1,128)}, u32[]{:S(2)}) copy-start(f32[512,1,96]{2,1,0:T(1,128)} %get-tuple-element.142) | copy-start | bytes 589828
  584.3 13.6 %copy-start.19 = (f32[64,8,96]{2,0,1:T(8,128)S(1)}, f32[64,8,96]{2,0,1:T(8,128)}, u32[]{:S(2)}) copy-start(f32[64,8,96]{2,0,1:T(8,128)} %copy-done.18) | copy-start | bytes 589828
  584.3 13.6 %copy-start.21 = (f32[64,8,96]{2,0,1:T(8,128)S(1)}, f32[64,8,96]{2,0,1:T(8,128)}, u32[]{:S(2)}) copy-start(f32[64,8,96]{2,0,1:T(8,128)} %copy-done.20) | copy-start | bytes 589828
  585.0 12.9 %copy-start.15 = (f32[64,8,96]{2,0,1:T(8,128)S(1)}, f32[64,8,96]{2,0,1:T(8,128)}, u32[]{:S(2)}) copy-start(f32[64,8,96]{2,0,1:T(8,128)} %copy-done.14) | copy-start | bytes 589828
  585.0 12.9 %copy-start.17 = (f32[64,8,96]{2,0,1:T(8,128)S(1)}, f32[64,8,96]{2,0,1:T(8,128)}, u32[]{:S(2)}) copy-start(f32[64,8,96]{2,0,1:T(8,128)} %copy-done.16) | copy-start | bytes 589828
  585.8 12.1 %copy-start.7 = (f32[64,8,16,96]{3,2,0,1:T(8,128)S(1)}, f32[64,8,16,96]{3,2,0,1:T(8,128)}, u32[]{:S(2)}) copy-start(f32[64,8,16,96]{3,2,0,1:T(8,128)} %add_dynamic-update-slice_fusion) | copy-start | bytes 9437188
  585.8 12.1 %copy-start.8 = (f32[64,8,16,96]{3,2,0,1:T(8,128)S(1)}, f32[64,8,16,96]{3,2,0,1:T(8,128)}, u32[]{:S(2)}) copy-start(f32[64,8,16,96]{3,2,0,1:T(8,128)} %get-tuple-element.113) | copy-start | bytes 9437188
  (104 other events, 803.6 us)
Sparse Core Ops, SparseCore 0:
  102.3 153.9 all-reduce.1
where the time goes:
time: 793 us; the launch traced here: 780 us
  other arithmetic  264 us (33%)
  local copies, waits for them, and re-layouts  165 us (21%)
  waiting for transfers between devices  151 us (19%)
  blocking collectives  150 us (19%)
  starting transfers between devices  27 us (3%)
  between operations  15.7 us (2%)
    psum x1, waiting for transfers between devices, shards(): projected = lax.psum(partial_sums, 'space')  147 us
    all_gather x2, blocking collectives, entering_2(): gathered = jax.tree.map(lambda a: lax.all_gather(a, axis), part)  104 us
    another operation x1, other arithmetic, shards(): local_sum = jnp.cumsum(step_blocks, axis=1)  68.3 us
    reduce_sum x6, other arithmetic, shards(): results.append(jnp.sum(out_blocks[:, offset, :, None] * state_now, axis=1))  65.3 us
    unnamed x24, other arithmetic  55 us
    all_to_all x1, blocking collectives, shards(): lax.all_to_all(outgoing, 'space', split_axis=1, concat_axis=2, tiled=True)  47 us
    unnamed x324, local copies, waits for them, and re-layouts  35.1 us
    mul x36, local copies, waits for them, and re-layouts, weighted_inputs(): reach[:, None, :] * rate[None]  27 us
  transfers between devices with their start and end apart: 4, of which 2 were waited for; matrix products, arithmetic and copies ran while one was open for 4% of the time, Pallas kernels for 0%

commit v1 on v0

v1 whole, which is shorter than its diff:
```python
import jax
import jax.numpy as jnp
from jax import lax
from jax.experimental import pallas as pl
from jax.experimental.pallas import tpu as pltpu
from jax.sharding import PartitionSpec as P

MESH = pl.DeviceIdType.MESH
NS = 16
DTR = 48
KC = 4
BLK = 128
NBF = 32
DI = 1536
D = 768
TOK = 256
CH = 96
LANES = 128
TILES = DI // LANES
CHUNKS = 8
STEPS = TOK // CHUNKS
WROWS = 24
TROWS = 48
WB = DTR + DTR + 2 * NS
SEATS = 8
VMEM_LIMIT = 56 * 1024 * 1024
LOG2E = 1.4426950408889634
F32 = jnp.float32
BF16 = jnp.bfloat16


def scan_rows():
    r = lax.broadcasted_iota(jnp.int32, (TOK, TOK), 0)
    i = lax.broadcasted_iota(jnp.int32, (TOK, TOK), 1)
    return ((r % CHUNKS) * STEPS + r // CHUNKS == i).astype(F32).astype(BF16)


def token_rows():
    i = lax.broadcasted_iota(jnp.int32, (TOK, TOK), 0)
    r = lax.broadcasted_iota(jnp.int32, (TOK, TOK), 1)
    return ((r % CHUNKS) * STEPS + r // CHUNKS == i).astype(F32).astype(BF16)


def silu(v):
    half = 0.5 * v
    return half + half * jnp.tanh(half)


def lanes_of(tile, width=LANES):
    return pl.ds(pl.multiple_of(tile * width, width), width)


def spread_columns(projected, first, out):
    for n in range(NS):
        out[n] = jnp.broadcast_to(projected[:, first + n : first + n + 1], (TOK, LANES))


def layer(
    x, z, cw, cb, pwt, sw, sb, dl, sg, ow, order, out,
    xv, zv, owv, gwf, gwb, gt, tstage, tsend, trecv, where_to,
    wfa, wba, xf, sigt, gz, signal, step, rate2, rate_own, in_b, out_b, inner, reach, y, gated, grown,
    sends, recv, scan_e, scan_p, pk1, got1, pk2, got2, bsend, back,
    local, s1, r1, s2, r2, st, rt, sa, ra, sb1, rb1, sc, rc, sd, rd,
):
    f = lax.axis_index("tm")
    s = lax.axis_index("space")
    frames = lax.axis_size("tm")
    width = lax.axis_size("space")
    outer = frames // SEATS
    row = s // 4
    side = s // 2 % 2
    core = s % 2
    part = f // SEATS
    seat = f % SEATS
    sibling = (f, s - core + 1 - core)
    ahead = ((f + 1) % frames, s)
    behind = ((f + frames - 1) % frames, s)
    full = (CHUNKS, LANES)
    slot = (3, CHUNKS, LANES)
    sub = lax.broadcasted_iota(jnp.int32, full, 0)
    sub3 = lax.broadcasted_iota(jnp.int32, slot, 1)
    zero = jnp.zeros(full, F32)

    def near(d):
        return part * SEATS + (seat + d) % SEATS

    def far(d):
        return ((part + d) % outer) * SEATS + seat

    def remote(src, dst, ssem, rsem, target):
        return pltpu.make_async_remote_copy(
            src_ref=src,
            dst_ref=dst,
            send_sem=ssem,
            recv_sem=rsem,
            device_id=target,
            device_id_type=MESH,
        )

    def push(src, dst, ssem, rsem, target):
        copy = remote(src, dst, ssem, rsem, target)
        copy.start()
        return copy

    load_x = pltpu.make_async_copy(x, xv, local.at[0])
    load_z = pltpu.make_async_copy(z, zv, local.at[1])
    load_ow = pltpu.make_async_copy(ow, owv, local.at[2])
    load_x.start()

    barrier = pltpu.get_barrier_semaphore()
    for d in range(1, width):
        pl.semaphore_signal(barrier, inc=1, device_id=(f, (s + d) % width), device_id_type=MESH)
    for d in range(1, SEATS):
        pl.semaphore_signal(barrier, inc=1, device_id=(near(d), s), device_id_type=MESH)
    for d in range(1, outer):
        pl.semaphore_signal(barrier, inc=1, device_id=(far(d), s), device_id_type=MESH)
    pl.semaphore_signal(barrier, inc=1, device_id=behind, device_id_type=MESH)

    load_z.start()
    load_ow.start()
    gwf[s, 0:KC] = cw[...]
    gwf[s, KC : KC + 1] = cb[...]
    gwf[s, 5:6] = sb[...]
    gwf[s, 6:7] = sg[...]
    gwf[s, 7:8] = jnp.zeros((1, CH), F32)
    gwf[s, 8:WROWS] = dl[...]
    gwb[s, 0:DTR] = sw[...]
    gwb[s, DTR:WB] = pwt[...]
    tstage[...] = jnp.zeros_like(tstage)
    load_x.wait()
    for b in range(2):
        ends = xv[BLK * (b + 1) - 16 : BLK * (b + 1)].astype(F32)
        for t in range(KC - 1):
            for j in range(TILES):
                line = ends[13 + t : 14 + t, LANES * j : LANES * (j + 1)]
                tstage[b, t * TILES + j : t * TILES + j + 1] = line
    gt[pl.ds(2 * s, 2)] = tstage[...].astype(BF16)
    pl.semaphore_wait(barrier, width + SEATS + outer - 2)

    def chip(dx, dy):
        return (row + dx) % 4 * 4 + (side + dy) % 2 * 2 + core

    def place(a, i):
        return (gwf.at[i], gt.at[pl.ds(2 * i, 2)], gwb.at[i])[a]

    sent = []
    relayed = [0, 0, 0]

    def relay(a, dx, dy, tx, ty):
        ref = place(a, chip(dx, dy))
        landing = (dx - tx) % 4 * 2 + (dy - ty) % 2
        ssem = s1.at[a, relayed[a]]
        relayed[a] += 1
        sent.append(push(ref, ref, ssem, r1.at[a, landing], (f, chip(tx, ty))))

    def share(a, dx, dy):
        ref = place(a, chip(dx, dy))
        k = dx * 2 + dy
        sent.append(push(ref, ref, s2.at[a, k], r2.at[a, k], sibling))

    def take(a, dx, dy):
        ref = place(a, chip(dx, dy))
        remote(ref, ref, s1.at[a, 0], r1.at[a, dx * 2 + dy], sibling).wait_recv()

    def own_item(a):
        relay(a, 0, 0, 1, 0)
        relay(a, 0, 0, 3, 0)
        relay(a, 0, 0, 0, 1)
        share(a, 0, 0)

    def other_side(a):
        take(a, 0, 1)
        relay(a, 0, 1, 1, 0)
        relay(a, 0, 1, 3, 0)
        share(a, 0, 1)

    def neighbours(a):
        came, onward = ((1, 3), (1, 3), (3, 1))[a]
        for dy in range(2):
            take(a, came, dy)
            relay(a, came, dy, onward, 0)
            share(a, came, dy)
        for dy in range(2):
            take(a, onward, dy)
            share(a, onward, dy)

    def opposite(a):
        for dy in range(2):
            take(a, 2, dy)
            share(a, 2, dy)

    def from_sibling(a):
        for dx in range(4):
            for dy in range(2):
                ref = place(a, chip(dx, dy) - core + 1 - core)
                k = dx * 2 + dy
                remote(ref, ref, s2.at[a, k], r2.at[a, k], sibling).wait_recv()

    for a in range(3):
        own_item(a)
    listed = [order[j] for j in range(NBF)]

    def inverse(r, carry):
        found = 0
        for j in range(NBF):
            found = jnp.where(listed[j] == r, j, found)
        where_to[r] = found
        return carry

    lax.fori_loop(0, NBF, inverse, 0)
    for b in range(2):
        xf[b, 0:8] = jnp.zeros((8, DI), F32)

    def widen(tile, carry):
        lanes = lanes_of(tile)
        for b in range(2):
            xf[b, 8 : 8 + BLK, lanes] = xv[BLK * b : BLK * (b + 1), lanes].astype(F32)
        return carry

    lax.fori_loop(0, TILES, widen, 0)
    sends[...] = jnp.zeros_like(sends)
    other_side(0)
    other_side(1)
    neighbours(0)
    opposite(0)
    neighbours(1)
    other_side(2)
    from_sibling(0)
    for i in range(DI // CH):
        wfa[:, CH * i : CH * (i + 1)] = gwf[i]

    def filtered(b, count, lanes):
        total = wfa[4:5, lanes]
        for k in range(KC):
            total = total + wfa[k : k + 1, lanes] * xf[b, 5 + k : 5 + k + count, lanes]
        return silu(total).astype(BF16)

    def convolve(tile, carry):
        lanes = lanes_of(tile)
        for b in range(2):
            sigt[BLK * b : BLK * (b + 1), lanes] = filtered(b, BLK, lanes)
        return carry

    lax.fori_loop(0, 3, convolve, 0)
    opposite(1)
    neighbours(2)
    lax.fori_loop(3, 6, convolve, 0)
    from_sibling(1)
    tsend[...] = gt[order[NBF - 1]]
    sent_tail = push(tsend, trecv, st, rt, ahead)
    sent.append(sent_tail)
    opposite(2)
    lax.fori_loop(6, TILES, convolve, 0)
    rate2[...] = -jnp.exp(wfa[8:WROWS]) * LOG2E
    rearranged = scan_rows()
    load_z.wait()

    def gate(chunk, carry):
        lanes = lanes_of(chunk, 256)
        zs = jnp.dot(rearranged, zv[:, lanes], preferred_element_type=F32)
        gz[:, lanes] = silu(zs)
        return carry

    lax.fori_loop(0, DI // 256, gate, 0)
    from_sibling(2)
    for i in range(DI // CH):
        wba[:, CH * i : CH * (i + 1)] = gwb[i].astype(F32)
    sent_tail.wait_recv()
    came = trecv[...].astype(F32)
    opening = jnp.full(came.shape, f, jnp.int32) == 0
    gt[NBF] = jnp.where(opening, 0.0, came).astype(BF16)
    for b in range(2):
        at = where_to[2 * s + b]
        before = jnp.where(at == 0, NBF, order[jnp.maximum(at - 1, 0)])
        halo = gt[before].astype(F32)
        for t in range(KC - 1):
            for j in range(TILES):
                line = halo[t * TILES + j : t * TILES + j + 1]
                xf[b, 5 + t : 6 + t, LANES * j : LANES * (j + 1)] = line

    def heads(tile, carry):
        lanes = lanes_of(tile)
        for b in range(2):
            sigt[BLK * b : BLK * b + 16, lanes] = filtered(b, 16, lanes)
        return carry

    lax.fori_loop(0, TILES, heads, 0)

    def rearrange(chunk, carry):
        lanes = lanes_of(chunk, 256)
        signal[:, lanes] = jnp.dot(rearranged, sigt[:, lanes], preferred_element_type=F32)
        return carry

    lax.fori_loop(0, DI // 256, rearrange, 0)
    proj = lax.dot_general(
        signal[...].astype(BF16),
        wba[DTR:WB].astype(BF16),
        (((1,), (1,)), ((), ())),
        preferred_element_type=F32,
    )
    spread_columns(proj, DTR, in_b)
    rank = proj[:, :DTR]
    high = rank.astype(BF16)
    rest = rank - high.astype(F32)
    mid = rest.astype(BF16)
    low = (rest - mid.astype(F32)).astype(BF16)

    def steps(chunk, carry):
        lanes = lanes_of(chunk, 256)
        weight = wba[0:DTR, lanes].astype(BF16)
        total = wfa[5:6, lanes] + jnp.dot(low, weight, preferred_element_type=F32)
        total = total + jnp.dot(mid, weight, preferred_element_type=F32)
        total = total + jnp.dot(high, weight, preferred_element_type=F32)
        step[:, lanes] = jnp.maximum(total, 0.0) + jnp.log1p(jnp.exp(-jnp.abs(total)))
        return carry

    lax.fori_loop(0, DI // 256, steps, 0)
    m1 = sub % 4 >= 1
    m2 = sub % 4 >= 2

    def rows_of(t):
        return pl.ds(pl.multiple_of(t * CHUNKS, CHUNKS), CHUNKS)

    def rates_of(lanes):
        return [jnp.broadcast_to(rate2[n : n + 1, lanes], full) for n in range(NS)]

    def block_states(tile, carry):
        lanes = lanes_of(tile)
        rates = rates_of(lanes)

        def one(t, held):
            states, total = held
            rows = rows_of(t)
            now = step[rows, lanes]
            drive = now * signal[rows, lanes]
            states = tuple(
                jnp.exp2(now * rates[n]) * states[n] + in_b[n, rows, :] * drive for n in range(NS)
            )
            return states, total + now

        states, total = lax.fori_loop(0, STEPS, one, ((zero,) * NS, zero), unroll=4)
        sum1 = total + jnp.where(m1, pltpu.roll(total, 1, 0), 0.0)
        sum2 = sum1 + jnp.where(m2, pltpu.roll(sum1, 2, 0), 0.0)
        reach[:, lanes] = jnp.where(m1, pltpu.roll(sum2, 1, 0), 0.0)
        ends = jnp.where(
            sub < 4, jnp.broadcast_to(sum2[3:4], full), jnp.broadcast_to(sum2[7:8], full)
        )
        group = tile // 3
        place = tile % 3
        for h in range(4):
            state_out = zero
            rate_out = zero
            for q in range(4):
                n = 4 * h + q
                decay = jnp.exp2(rates[n] * total)
                one_s = states[n] + jnp.where(m1, decay * pltpu.roll(states[n], 1, 0), 0.0)
                decay2 = jnp.exp2(rates[n] * sum1)
                two_s = one_s + jnp.where(m2, decay2 * pltpu.roll(one_s, 2, 0), 0.0)
                inner[n, :, lanes] = jnp.where(m1, pltpu.roll(two_s, 1, 0), 0.0)
                turn = (q + 5) % 8
                moved = pltpu.roll(two_s, turn, 0) if turn else two_s
                state_out = jnp.where(sub % 4 == q, moved, state_out)
                rate_out = jnp.where(sub % 4 == q, rates[n], rate_out)
            sends[group * 4 + h, place] = state_out
            sends[group * 4 + h, 3] = jnp.where(sub % 4 == place, ends, sends[group * 4 + h, 3])
            rate_own[h, tile] = rate_out
        return carry

    def to_owner(peer):
        return remote(sends.at[peer], recv.at[s], sa.at[peer], ra.at[s], (f, peer))

    def one_group(g, carry):
        lax.fori_loop(g * 3, g * 3 + 3, block_states, 0)
        for h in range(4):
            peer = g * 4 + h

            @pl.when(peer != s)
            def _():
                to_owner(peer).start()

        return carry

    lax.fori_loop(0, 4, one_group, 0)
    recv[s] = sends[s]
    spread_columns(proj, DTR + NS, out_b)

    def own_outputs(tile, carry):
        lanes = lanes_of(tile)
        rates = rates_of(lanes)
        skip = jnp.broadcast_to(wfa[6:7, lanes], full)

        def one(t, held):
            states, total = held
            rows = rows_of(t)
            now = step[rows, lanes]
            sig = signal[rows, lanes]
            drive = now * sig
            total = total + now
            states = tuple(
                jnp.exp2(now * rates[n]) * states[n] + in_b[n, rows, :] * drive for n in range(NS)
            )
            coeffs = [out_b[n, rows, :] for n in range(NS)]
            terms = [coeffs[n] * states[n] for n in range(NS)]
            for n in range(NS):
                grown[n, rows, lanes] = coeffs[n] * jnp.exp2(total * rates[n])
            while len(terms) > 1:
                terms = [a + b for a, b in zip(terms[::2], terms[1::2])]
            y[rows, lanes] = terms[0] + skip * sig
            return states, total

        states = tuple(inner[n, :, lanes] for n in range(NS))
        lax.fori_loop(0, STEPS, one, (states, reach[:, lanes]), unroll=2)
        return carry

    lax.fori_loop(0, 3, own_outputs, 0)
    for d in range(1, width):
        peer = (s + d) % width
        remote(sends.at[peer], recv.at[peer], sa.at[peer], ra.at[peer], (f, peer)).wait_recv()

    def turned(v):
        return pltpu.roll(v, 4, len(v.shape) - 2)

    my_group = s // 4
    my_rates = rate_own[s % 4, pl.ds(my_group * 3, 3)]

    def through(j, carry):
        e, p = carry
        scan_e[j] = e
        scan_p[j] = p
        block = order[j]
        got = recv[lax.shift_right_logical(block, 1)]
        odd = jnp.full((4, CHUNKS, LANES), block & 1, jnp.int32) == 1
        got = jnp.where(odd, turned(got), got)
        sums = jnp.stack([jnp.broadcast_to(got[3, i : i + 1], full) for i in range(3)])
        a = jnp.exp2(my_rates * sums)
        return a * e + got[0:3], a * p

    zero3 = jnp.zeros(slot, F32)
    unit3 = jnp.ones(slot, F32)
    e, p = lax.fori_loop(0, NBF, through, (zero3, unit3), unroll=8)
    pk1[...] = jnp.where(sub3 < 4, p, turned(e))
    got1[seat] = pk1[...]
    level1 = []
    for d in range(1, SEATS):
        level1.append(push(pk1, got1.at[seat], sb1.at[d], rb1.at[d], (near(d), s)))
    lax.fori_loop(3, 6, own_outputs, 0)
    for copy in level1:
        copy.wait_recv()

    def gather_near(m, carry):
        e_in, p_in, e_all, p_all = carry
        got = got1[m]
        moved = turned(got)
        early = jnp.full(slot, m, jnp.int32) < jnp.full(slot, seat, jnp.int32)
        e_in = jnp.where(early, got * e_in + moved, e_in)
        p_in = jnp.where(early, got * p_in, p_in)
        return e_in, p_in, got * e_all + moved, got * p_all

    begin = (zero3, unit3, zero3, unit3)
    e_in, p_in, e_all, p_all = lax.fori_loop(0, SEATS, gather_near, begin, unroll=SEATS)
    pk2[...] = jnp.where(sub3 < 4, p_all, turned(e_all))
    got2[part] = pk2[...]
    level2 = []
    for d in range(1, outer):
        level2.append(push(pk2, got2.at[part], sc.at[d], rc.at[d], (far(d), s)))
    lax.fori_loop(6, 9, own_outputs, 0)
    for copy in level2:
        copy.wait_recv()

    def gather_far(m, start):
        got = got2[m]
        early = jnp.full(slot, m, jnp.int32) < jnp.full(slot, part, jnp.int32)
        return jnp.where(early, got * start + turned(got), start)

    start = lax.fori_loop(0, outer, gather_far, zero3, unroll=4)
    start = p_in * start + e_in

    def pack(d, carry):
        i0 = where_to[2 * d]
        i1 = where_to[2 * d + 1]
        even = scan_e[i0] + scan_p[i0] * start
        odd = scan_e[i1] + scan_p[i1] * start
        bsend[d] = jnp.where(sub3 < 4, even, turned(odd))
        return carry

    lax.fori_loop(0, width, pack, 0, unroll=4)
    back[s] = bsend[s]
    returns = []
    for d in range(1, width):
        peer = (s + d) % width
        returns.append(push(bsend.at[peer], back.at[s], sd.at[peer], rd.at[s], (f, peer)))
    lax.fori_loop(9, 12, own_outputs, 0)
    load_ow.wait()
    def complete(tile, carry):
        lanes = lanes_of(tile)
        group = tile // 3
        place = tile % 3
        entering = []
        for n in range(NS):
            came = back[group * 4 + n // 4, place]
            q = n % 4
            entering.append(
                jnp.where(
                    sub < 4,
                    jnp.broadcast_to(came[q : q + 1], full),
                    jnp.broadcast_to(came[4 + q : 5 + q], full),
                )
            )

        def one(t, carry):
            rows = rows_of(t)
            terms = [grown[n, rows, lanes] * entering[n] for n in range(NS)]
            while len(terms) > 1:
                terms = [a + b for a, b in zip(terms[::2], terms[1::2])]
            scanned = (y[rows, lanes] + terms[0]).astype(BF16).astype(F32)
            y[rows, lanes] = scanned * gz[rows, lanes]
            return carry

        lax.fori_loop(0, STEPS, one, 0, unroll=4)
        gated[:, lanes] = y[:, lanes].astype(BF16)
        return carry

    def one_return(g, carry):
        for h in range(4):
            peer = g * 4 + h

            @pl.when(peer != s)
            def _():
                remote(
                    bsend.at[peer], back.at[peer], sd.at[peer], rd.at[peer], (f, peer)
                ).wait_recv()

        lax.fori_loop(g * 3, g * 3 + 3, complete, 0)
        return carry

    lax.fori_loop(0, 4, one_return, 0)
    undo = token_rows()

    def mix(chunk, carry):
        lanes = lanes_of(chunk, 256)
        mixed = jnp.dot(gated[...], owv[:, lanes], preferred_element_type=F32).astype(BF16)
        out[:, lanes] = jnp.dot(undo, mixed, preferred_element_type=F32).astype(BF16)
        return carry

    lax.fori_loop(0, D // 256, mix, 0)
    for copy in sent + level1 + level2 + returns:
        copy.wait_send()
    for d in range(1, width):
        to_owner((s + d) % width).wait_send()


def shards(
    inner_x,
    inner_z,
    conv_weight,
    conv_bias,
    proj_weight,
    step_weight,
    step_bias,
    decay_log,
    skip_gain,
    out_weight,
    order_table,
):
    frames, rows, columns, channels = inner_x.shape
    space = lax.axis_size("space")
    outer = lax.axis_size("tm") // SEATS
    dma = pltpu.SemaphoreType.DMA
    slot = (3, CHUNKS, LANES)
    anyw = pl.BlockSpec(memory_space=pl.ANY)
    vm = pl.BlockSpec(memory_space=pltpu.VMEM)
    held = [
        ((TOK, DI), BF16),
        ((TOK, DI), BF16),
        ((DI, D), BF16),
        ((space, WROWS, CH), F32),
        ((space, WB, CH), BF16),
        ((NBF + 1, TROWS, LANES), BF16),
        ((2, TROWS, LANES), F32),
        ((TROWS, LANES), BF16),
        ((TROWS, LANES), BF16),
        None,
        ((WROWS, DI), F32),
        ((WB, DI), F32),
        ((2, BLK + 8, DI), F32),
        ((TOK, DI), BF16),
        ((TOK, DI), F32),
        ((TOK, DI), F32),
        ((TOK, DI), F32),
        ((NS, DI), F32),
        ((4, TILES, CHUNKS, LANES), F32),
        ((NS, TOK, LANES), F32),
        ((NS, TOK, LANES), F32),
        ((NS, CHUNKS, DI), F32),
        ((CHUNKS, DI), F32),
        ((TOK, DI), F32),
        ((TOK, DI), BF16),
        ((NS, TOK, DI), F32),
        ((space, 4, CHUNKS, LANES), F32),
        ((space, 4, CHUNKS, LANES), F32),
        ((NBF,) + slot, F32),
        ((NBF,) + slot, F32),
        (slot, F32),
        ((SEATS,) + slot, F32),
        (slot, F32),
        ((outer,) + slot, F32),
        ((space,) + slot, F32),
        ((space,) + slot, F32),
    ]
    scratch = [pltpu.SMEM((NBF,), jnp.int32) if h is None else pltpu.VMEM(*h) for h in held]
    scratch += [dma((3,))] + [dma((3, 8))] * 4 + [dma] * 2
    scratch += [dma((16,))] * 2 + [dma((8,))] * 4 + [dma((16,))] * 2
    out = pl.pallas_call(
        layer,
        out_shape=jax.ShapeDtypeStruct((TOK, D), BF16),
        in_specs=[anyw, anyw] + [vm] * 7 + [anyw, pl.BlockSpec(memory_space=pltpu.SMEM)],
        out_specs=vm,
        scratch_shapes=scratch,
        compiler_params=pltpu.CompilerParams(
            collective_id=0, has_side_effects=True, vmem_limit_bytes=VMEM_LIMIT
        ),
        name="layer",
    )(
        inner_x.reshape(TOK, DI),
        inner_z.reshape(TOK, DI),
        conv_weight,
        conv_bias.reshape(1, CH),
        proj_weight.T,
        step_weight,
        step_bias.reshape(1, CH),
        decay_log,
        skip_gain.reshape(1, CH),
        out_weight,
        order_table,
    )
    return out.reshape(frames, rows, columns, D)


def solution(mesh):
    in_specs = (
        P("tm", "space", None, None),
        P("tm", "space", None, None),
        P(None, "space"),
        P("space"),
        P("space", None),
        P(None, "space"),
        P("space"),
        P(None, "space"),
        P("space"),
        P(),
        P(),
    )
    out_specs = P("tm", "space", None, None)
    return jax.shard_map(shards, mesh=mesh, in_specs=in_specs, out_specs=out_specs, check_vma=False)
```

time: 793 us -> 76.5 us (0.10)
  the two profiles are of different devices: /device:TPU:489 before, /device:TPU:1 now
where the time goes in v1:
time: 76.5 us; the launch traced here: 76.2 us
  Pallas kernels  74.5 us (97%)
  local copies, waits for them, and re-layouts  1.77 us (2%)
    pallas_call x1, Pallas kernels, shards(): pl.pallas_call(layer, out_shape=jax.ShapeDtypeStruct((TOK, D), BF16), in_...  74.5 us
    unnamed x1, local copies, waits for them, and re-layouts  1.77 us

profile of v1, /device:TPU:1, one launch (start us, length us, event | category | flops | bytes accessed | tf_op | source)
XLA Modules:
  0.0 76.2 jit_solution(9492186474825221465)
XLA Ops:
  0.0 74.5 %layer.1 = bf16[256,768]{1,0:T(8,128)(2,1)} custom-call(bf16[256,1536]{1,0:T(8,128)(2,1)} %bitcast.8, bf16[256,1536]{1,0:T(8,128)(2,1)} %bitcast.9, f32[4,96]{1,0:T(4,128)} %cw.1, f32[1,96]{1,0:T(1,128)} %bitcast.11, bf16[80,96]{1,0:T(8,128)(2,1)} %bitcast.10, bf16[48,96]{1,0:T(8,128)(2,1)} %sw.1, f32[1,96]{1,0:T(1,128)} %bitcast.12, f32[16,96]{1,0:T(8,128)} %dl.1, ...), custom_call_target="tpu_custom_call" | custom-call | tf_op jit(solution)/shard_map/layer/pallas_call | solution.py:613
  74.5 1.8 %copy.13 = bf16[1,4,64,768]{3,2,1,0:T(8,128)(2,1)} copy(bf16[1,4,64,768]{3,2,1,0:T(8,128)(2,1)} %bitcast.7) | data formatting | bytes 786432

commit v2 on v1

--- a/solution.py
+++ b/solution.py
@@ -32,13 +32,13 @@
 def scan_rows():
     r = lax.broadcasted_iota(jnp.int32, (TOK, TOK), 0)
     i = lax.broadcasted_iota(jnp.int32, (TOK, TOK), 1)
-    return ((r % CHUNKS) * STEPS + r // CHUNKS == i).astype(F32).astype(BF16)
+    return ((r & (CHUNKS - 1)) * STEPS + (r >> 3) == i).astype(F32).astype(BF16)
 
 
 def token_rows():
     i = lax.broadcasted_iota(jnp.int32, (TOK, TOK), 0)
     r = lax.broadcasted_iota(jnp.int32, (TOK, TOK), 1)
-    return ((r % CHUNKS) * STEPS + r // CHUNKS == i).astype(F32).astype(BF16)
+    return ((r & (CHUNKS - 1)) * STEPS + (r >> 3) == i).astype(F32).astype(BF16)
 
 
 def silu(v):
@@ -56,11 +56,11 @@
 
 
 def layer(
-    x, z, cw, cb, pwt, sw, sb, dl, sg, ow, order, out,
-    xv, zv, owv, gwf, gwb, gt, tstage, tsend, trecv, where_to,
+    x, z, cw, cb, pwt, sw, sb, dl, sg, order, out,
+    xv, zv, gwf, gwb, gt, tstage, tsend, trecv, where_to,
     wfa, wba, xf, sigt, gz, signal, step, rate2, rate_own, in_b, out_b, inner, reach, y, gated, grown,
-    sends, recv, scan_e, scan_p, pk1, got1, pk2, got2, bsend, back,
-    local, s1, r1, s2, r2, st, rt, sa, ra, sb1, rb1, sc, rc, sd, rd,
+    sends, recv, scan_e, scan_t, pk1, got1, pk2, got2, bsend, back, fsend, fback,
+    local, s1, r1, s2, r2, st, rt, sa, ra, sb1, rb1, sc, rc, sd, rd, sf, rf,
 ):
     f = lax.axis_index("tm")
     s = lax.axis_index("space")
@@ -73,6 +73,7 @@
     part = f // SEATS
     seat = f % SEATS
     sibling = (f, s - core + 1 - core)
+    twin = f + 1 - f % 2 * 2
     ahead = ((f + 1) % frames, s)
     behind = ((f + frames - 1) % frames, s)
     full = (CHUNKS, LANES)
@@ -80,6 +81,9 @@
     sub = lax.broadcasted_iota(jnp.int32, full, 0)
     sub3 = lax.broadcasted_iota(jnp.int32, slot, 1)
     zero = jnp.zeros(full, F32)
+
+    def chip(dx, dy):
+        return (row + dx) % 4 * 4 + (side + dy) % 2 * 2 + core
 
     def near(d):
         return part * SEATS + (seat + d) % SEATS
@@ -104,7 +108,6 @@
 
     load_x = pltpu.make_async_copy(x, xv, local.at[0])
     load_z = pltpu.make_async_copy(z, zv, local.at[1])
-    load_ow = pltpu.make_async_copy(ow, owv, local.at[2])
     load_x.start()
 
     barrier = pltpu.get_barrier_semaphore()
@@ -115,9 +118,10 @@
     for d in range(1, outer):
         pl.semaphore_signal(barrier, inc=1, device_id=(far(d), s), device_id_type=MESH)
     pl.semaphore_signal(barrier, inc=1, device_id=behind, device_id_type=MESH)
+    for dx in range(4):
+        pl.semaphore_signal(barrier, inc=1, device_id=(twin, chip(dx, 1)), device_id_type=MESH)
 
     load_z.start()
-    load_ow.start()
     gwf[s, 0:KC] = cw[...]
     gwf[s, KC : KC + 1] = cb[...]
     gwf[s, 5:6] = sb[...]
@@ -135,10 +139,7 @@
                 line = ends[13 + t : 14 + t, LANES * j : LANES * (j + 1)]
                 tstage[b, t * TILES + j : t * TILES + j + 1] = line
     gt[pl.ds(2 * s, 2)] = tstage[...].astype(BF16)
-    pl.semaphore_wait(barrier, width + SEATS + outer - 2)
-
-    def chip(dx, dy):
-        return (row + dx) % 4 * 4 + (side + dy) % 2 * 2 + core
+    pl.semaphore_wait(barrier, width + SEATS + outer + 2)
 
     def place(a, i):
         return (gwf.at[i], gt.at[pl.ds(2 * i, 2)], gwb.at[i])[a]
@@ -151,7 +152,8 @@
         landing = (dx - tx) % 4 * 2 + (dy - ty) % 2
         ssem = s1.at[a, relayed[a]]
         relayed[a] += 1
-        sent.append(push(ref, ref, ssem, r1.at[a, landing], (f, chip(tx, ty))))
+        frame = twin if ty and a != 1 else f
+        sent.append(push(ref, ref, ssem, r1.at[a, landing], (frame, chip(tx, ty))))
 
     def share(a, dx, dy):
         ref = place(a, chip(dx, dy))
@@ -161,6 +163,16 @@
     def take(a, dx, dy):
         ref = place(a, chip(dx, dy))
         remote(ref, ref, s1.at[a, 0], r1.at[a, dx * 2 + dy], sibling).wait_recv()
+
+    def offer(a):
+        for tx, ty in ((1, 0), (3, 0), (0, 1), (1, 1), (3, 1), (2, 0), (2, 1)):
+            relay(a, 0, 0, tx, ty)
+        share(a, 0, 0)
+
+    def collect(a):
+        for dx, dy in ((3, 0), (1, 0), (0, 1), (3, 1), (1, 1), (2, 0), (2, 1)):
+            take(a, dx, dy)
+            share(a, dx, dy)
 
     def own_item(a):
         relay(a, 0, 0, 1, 0)
@@ -175,14 +187,13 @@
         share(a, 0, 1)
 
     def neighbours(a):
-        came, onward = ((1, 3), (1, 3), (3, 1))[a]
         for dy in range(2):
-            take(a, came, dy)
-            relay(a, came, dy, onward, 0)
-            share(a, came, dy)
+            take(a, 1, dy)
+            relay(a, 1, dy, 3, 0)
+            share(a, 1, dy)
         for dy in range(2):
-            take(a, onward, dy)
-            share(a, onward, dy)
+            take(a, 3, dy)
+            share(a, 3, dy)
 
     def opposite(a):
         for dy in range(2):
@@ -196,8 +207,9 @@
                 k = dx * 2 + dy
                 remote(ref, ref, s2.at[a, k], r2.at[a, k], sibling).wait_recv()
 
-    for a in range(3):
-        own_item(a)
+    offer(0)
+    offer(1)
+    own_item(2)
     listed = [order[j] for j in range(NBF)]
 
     def inverse(r, carry):
@@ -219,12 +231,9 @@
 
     lax.fori_loop(0, TILES, widen, 0)
     sends[...] = jnp.zeros_like(sends)
-    other_side(0)
-    other_side(1)
-    neighbours(0)
-    opposite(0)
-    neighbours(1)
+    collect(0)
     other_side(2)
+    collect(1)
     from_sibling(0)
     for i in range(DI // CH):
         wfa[:, CH * i : CH * (i + 1)] = gwf[i]
@@ -242,7 +251,6 @@
         return carry
 
     lax.fori_loop(0, 3, convolve, 0)
-    opposite(1)
     neighbours(2)
     lax.fori_loop(3, 6, convolve, 0)
     from_sibling(1)
@@ -423,26 +431,43 @@
     my_group = s // 4
     my_rates = rate_own[s % 4, pl.ds(my_group * 3, 3)]
 
+    def decays(sums):
+        spread = [jnp.broadcast_to(sums[i : i + 1], full) for i in range(3)]
+        return jnp.exp2(my_rates * jnp.stack(spread))
+
     def through(j, carry):
-        e, p = carry
+        e, passed = carry
         scan_e[j] = e
-        scan_p[j] = p
+        scan_t[j] = passed
         block = order[j]
         got = recv[lax.shift_right_logical(block, 1)]
         odd = jnp.full((4, CHUNKS, LANES), block & 1, jnp.int32) == 1
         got = jnp.where(odd, turned(got), got)
-        sums = jnp.stack([jnp.broadcast_to(got[3, i : i + 1], full) for i in range(3)])
-        a = jnp.exp2(my_rates * sums)
-        return a * e + got[0:3], a * p
+        return decays(got[3]) * e + got[0:3], passed + got[3]
 
     zero3 = jnp.zeros(slot, F32)
     unit3 = jnp.ones(slot, F32)
-    e, p = lax.fori_loop(0, NBF, through, (zero3, unit3), unroll=8)
+    e, passed = lax.fori_loop(0, NBF, through, (zero3, zero), unroll=8)
+    p = decays(passed)
     pk1[...] = jnp.where(sub3 < 4, p, turned(e))
     got1[seat] = pk1[...]
     level1 = []
     for d in range(1, SEATS):
         level1.append(push(pk1, got1.at[seat], sb1.at[d], rb1.at[d], (near(d), s)))
+
+    def pack(d, carry):
+        i0 = where_to[2 * d]
+        i1 = where_to[2 * d + 1]
+        bsend[d, 0:3] = jnp.where(sub3 < 4, scan_e[i0], turned(scan_e[i1]))
+        bsend[d, 3] = jnp.where(sub < 4, scan_t[i0], turned(scan_t[i1]))
+        return carry
+
+    lax.fori_loop(0, width, pack, 0, unroll=4)
+    back[s] = bsend[s]
+    returns = []
+    for d in range(1, width):
+        peer = (s + d) % width
+        returns.append(push(bsend.at[peer], back.at[s], sd.at[peer], rd.at[s], (f, peer)))
     lax.fori_loop(3, 6, own_outputs, 0)
     for copy in level1:
         copy.wait_recv()
@@ -475,37 +500,37 @@
     start = lax.fori_loop(0, outer, gather_far, zero3, unroll=4)
     start = p_in * start + e_in
 
-    def pack(d, carry):
-        i0 = where_to[2 * d]
-        i1 = where_to[2 * d + 1]
-        even = scan_e[i0] + scan_p[i0] * start
-        odd = scan_e[i1] + scan_p[i1] * start
-        bsend[d] = jnp.where(sub3 < 4, even, turned(odd))
-        return carry
-
-    lax.fori_loop(0, width, pack, 0, unroll=4)
-    back[s] = bsend[s]
-    returns = []
+    first = jnp.where(sub < 4, start[0], turned(start[1]))
+    fsend[...] = jnp.concatenate([first, start[2]], axis=0).astype(BF16)
+    fback[s] = fsend[...]
+    starts = []
     for d in range(1, width):
         peer = (s + d) % width
-        returns.append(push(bsend.at[peer], back.at[s], sd.at[peer], rd.at[s], (f, peer)))
+        starts.append(push(fsend, fback.at[s], sf.at[peer], rf.at[s], (f, peer)))
     lax.fori_loop(9, 12, own_outputs, 0)
-    load_ow.wait()
-    def complete(tile, carry):
-        lanes = lanes_of(tile)
-        group = tile // 3
-        place = tile % 3
+    for d in range(1, width):
+        peer = (s + d) % width
+        remote(bsend.at[peer], back.at[peer], sd.at[peer], rd.at[peer], (f, peer)).wait_recv()
+
+    def both(tile8, r):
+        return jnp.where(
+            sub < 4,
+            jnp.broadcast_to(tile8[r : r + 1], full),
+            jnp.broadcast_to(tile8[4 + r : 5 + r], full),
+        )
+
+    def complete(g, place):
+        lanes = lanes_of(g * 3 + place)
+        rates = rates_of(lanes)
+        passed = both(back[g * 4, 3], place)
         entering = []
-        for n in range(NS):
-            came = back[group * 4 + n // 4, place]
-            q = n % 4
-            entering.append(
-                jnp.where(
-                    sub < 4,
-                    jnp.broadcast_to(came[q : q + 1], full),
-                    jnp.broadcast_to(came[4 + q : 5 + q], full),
-                )
-            )
+        for h in range(4):
+            came = back[g * 4 + h, place]
+            begun = fback[g * 4 + h].astype(F32)
+            for q in range(4):
+                r = place * 4 + q
+                line = jnp.broadcast_to(begun[r : r + 1], full)
+                entering.append(both(came, q) + jnp.exp2(rates[4 * h + q] * passed) * line)
 
         def one(t, carry):
             rows = rows_of(t)
@@ -518,32 +543,25 @@
 
         lax.fori_loop(0, STEPS, one, 0, unroll=4)
         gated[:, lanes] = y[:, lanes].astype(BF16)
-        return carry
-
-    def one_return(g, carry):
+
+    undo = token_rows()
+
+    def one_group_back(g, carry):
         for h in range(4):
             peer = g * 4 + h
 
             @pl.when(peer != s)
             def _():
-                remote(
-                    bsend.at[peer], back.at[peer], sd.at[peer], rd.at[peer], (f, peer)
-                ).wait_recv()
-
-        lax.fori_loop(g * 3, g * 3 + 3, complete, 0)
-        return carry
-
-    lax.fori_loop(0, 4, one_return, 0)
-    undo = token_rows()
-
-    def mix(chunk, carry):
-        lanes = lanes_of(chunk, 256)
-        mixed = jnp.dot(gated[...], owv[:, lanes], preferred_element_type=F32).astype(BF16)
-        out[:, lanes] = jnp.dot(undo, mixed, preferred_element_type=F32).astype(BF16)
-        return carry
-
-    lax.fori_loop(0, D // 256, mix, 0)
-    for copy in sent + level1 + level2 + returns:
+                remote(fsend, fback.at[peer], sf.at[peer], rf.at[peer], (f, peer)).wait_recv()
+
+        for place in range(3):
+            complete(g, place)
+        lanes = lanes_of(g, 3 * LANES)
+        out[:, lanes] = jnp.dot(undo, gated[:, lanes], preferred_element_type=F32).astype(BF16)
+        return carry
+
+    lax.fori_loop(0, 4, one_group_back, 0)
+    for copy in sent + level1 + level2 + returns + starts:
         copy.wait_send()
     for d in range(1, width):
         to_owner((s + d) % width).wait_send()
@@ -572,7 +590,6 @@
     held = [
         ((TOK, DI), BF16),
         ((TOK, DI), BF16),
-        ((DI, D), BF16),
         ((space, WROWS, CH), F32),
         ((space, WB, CH), BF16),
         ((NBF + 1, TROWS, LANES), BF16),
@@ -599,21 +616,23 @@
         ((space, 4, CHUNKS, LANES), F32),
         ((space, 4, CHUNKS, LANES), F32),
         ((NBF,) + slot, F32),
-        ((NBF,) + slot, F32),
+        ((NBF, CHUNKS, LANES), F32),
         (slot, F32),
         ((SEATS,) + slot, F32),
         (slot, F32),
         ((outer,) + slot, F32),
-        ((space,) + slot, F32),
-        ((space,) + slot, F32),
+        ((space, 4, CHUNKS, LANES), F32),
+        ((space, 4, CHUNKS, LANES), F32),
+        ((16, LANES), BF16),
+        ((space, 16, LANES), BF16),
     ]
     scratch = [pltpu.SMEM((NBF,), jnp.int32) if h is None else pltpu.VMEM(*h) for h in held]
-    scratch += [dma((3,))] + [dma((3, 8))] * 4 + [dma] * 2
-    scratch += [dma((16,))] * 2 + [dma((8,))] * 4 + [dma((16,))] * 2
-    out = pl.pallas_call(
+    scratch += [dma((2,))] + [dma((3, 8))] * 4 + [dma] * 2
+    scratch += [dma((16,))] * 2 + [dma((8,))] * 4 + [dma((16,))] * 4
+    gated = pl.pallas_call(
         layer,
-        out_shape=jax.ShapeDtypeStruct((TOK, D), BF16),
-        in_specs=[anyw, anyw] + [vm] * 7 + [anyw, pl.BlockSpec(memory_space=pltpu.SMEM)],
+        out_shape=jax.ShapeDtypeStruct((TOK, DI), BF16),
+        in_specs=[anyw, anyw] + [vm] * 7 + [pl.BlockSpec(memory_space=pltpu.SMEM)],
         out_specs=vm,
         scratch_shapes=scratch,
         compiler_params=pltpu.CompilerParams(
@@ -630,10 +649,10 @@
         step_bias.reshape(1, CH),
         decay_log,
         skip_gain.reshape(1, CH),
-        out_weight,
         order_table,
     )
-    return out.reshape(frames, rows, columns, D)
+    mixed = jnp.dot(gated, out_weight, preferred_element_type=F32).astype(BF16)
+    return mixed.reshape(frames, rows, columns, D)
 
 
 def solution(mesh):

time: 76.5 us -> 72.4 us (0.946)
  Pallas kernels: 74.5 us -> 69.6 us
  matrix products: 0 us -> 2.66 us
  local copies, waits for them, and re-layouts: 1.77 us -> 0.01 us
    pallas_call x1, Pallas kernels: 74.5 us -> 69.6 us  [shards(): pl.pallas_call(layer, out_shape=jax.ShapeDtypeStruct((TOK, DI), BF16), in...]
    dot_general x0 -> x1, matrix products: none -> 2.66 us  [shards(): mixed = jnp.dot(gated, out_weight, preferred_element_type=F32).astype(BF16)]
    unnamed x1 -> x2, local copies, waits for them, and re-layouts: 1.77 us -> 0.01 us
where the time goes in v2:
time: 72.4 us; the launch traced here: 72.3 us
  Pallas kernels  69.6 us (96%)
  matrix products  2.66 us (4%)
    pallas_call x1, Pallas kernels, shards(): pl.pallas_call(layer, out_shape=jax.ShapeDtypeStruct((TOK, DI), BF16), in...  69.6 us
    dot_general x1, matrix products, shards(): mixed = jnp.dot(gated, out_weight, preferred_element_type=F32).astype(BF16)  2.66 us

profile of v2, /device:TPU:1, one launch (start us, length us, event | category | flops | bytes accessed | tf_op | source)
XLA Modules:
  0.0 72.3 jit_solution(14314632944063719473)
XLA Ops:
  0.0 0.0 copy-start
  0.0 69.6 %layer.1 = bf16[256,1536]{1,0:T(8,128)(2,1)} custom-call(bf16[256,1536]{1,0:T(8,128)(2,1)} %bitcast.9, bf16[256,1536]{1,0:T(8,128)(2,1)} %bitcast.10, f32[4,96]{1,0:T(4,128)} %cw.1, f32[1,96]{1,0:T(1,128)} %bitcast.12, bf16[80,96]{1,0:T(8,128)(2,1)} %bitcast.11, bf16[48,96]{1,0:T(8,128)(2,1)} %sw.1, f32[1,96]{1,0:T(1,128)} %bitcast.13, f32[16,96]{1,0:T(8,128)} %dl.1, ...), custom_call_target="tpu_custom_call" | custom-call | tf_op jit(solution)/shard_map/layer/pallas_call | solution.py:632
  69.6 0.0 copy-done
  69.6 2.7 %convolution_convert_fusion = bf16[256,768]{1,0:T(8,128)(2,1)} fusion(bf16[256,1536]{1,0:T(8,128)(2,1)} %layer.1, bf16[1536,768]{1,0:T(8,128)(2,1)S(1)} %copy-done), kind=kOutput, calls=%fused_computation | convolution fusion | flops 604176384 | bytes 3538944 | tf_op jit(solution)/shard_map/dot_general | solution.py:654
Async XLA Ops:
  0.0 69.6 %copy-start = (bf16[1536,768]{1,0:T(8,128)(2,1)S(1)}, bf16[1536,768]{1,0:T(8,128)(2,1)}, u32[]{:S(2)}) copy-start(bf16[1536,768]{1,0:T(8,128)(2,1)} %param.20) | copy-start | bytes 7077892

commit v3 on v2

--- a/solution.py
+++ b/solution.py
@@ -60,7 +60,7 @@
     xv, zv, gwf, gwb, gt, tstage, tsend, trecv, where_to,
     wfa, wba, xf, sigt, gz, signal, step, rate2, rate_own, in_b, out_b, inner, reach, y, gated, grown,
     sends, recv, scan_e, scan_t, pk1, got1, pk2, got2, bsend, back, fsend, fback,
-    local, s1, r1, s2, r2, st, rt, sa, ra, sb1, rb1, sc, rc, sd, rd, sf, rf,
+    local, s1, r1, s2, r2, st, rt, sa, ra, sb1, rb1, sc, rc, sd, rd, sf, rf, up, down,
 ):
     f = lax.axis_index("tm")
     s = lax.axis_index("space")
@@ -115,8 +115,10 @@
         pl.semaphore_signal(barrier, inc=1, device_id=(f, (s + d) % width), device_id_type=MESH)
     for d in range(1, SEATS):
         pl.semaphore_signal(barrier, inc=1, device_id=(near(d), s), device_id_type=MESH)
-    for d in range(1, outer):
-        pl.semaphore_signal(barrier, inc=1, device_id=(far(d), s), device_id_type=MESH)
+    above = ((f + 2) % frames, s)
+    below = ((f + frames - 2) % frames, s)
+    for neighbour in (above, below):
+        pl.semaphore_signal(barrier, inc=1, device_id=neighbour, device_id_type=MESH)
     pl.semaphore_signal(barrier, inc=1, device_id=behind, device_id_type=MESH)
     for dx in range(4):
         pl.semaphore_signal(barrier, inc=1, device_id=(twin, chip(dx, 1)), device_id_type=MESH)
@@ -139,7 +141,7 @@
                 line = ends[13 + t : 14 + t, LANES * j : LANES * (j + 1)]
                 tstage[b, t * TILES + j : t * TILES + j + 1] = line
     gt[pl.ds(2 * s, 2)] = tstage[...].astype(BF16)
-    pl.semaphore_wait(barrier, width + SEATS + outer + 2)
+    pl.semaphore_wait(barrier, width + SEATS + 5)
 
     def place(a, i):
         return (gwf.at[i], gt.at[pl.ds(2 * i, 2)], gwb.at[i])[a]
@@ -175,25 +177,18 @@
             share(a, dx, dy)
 
     def own_item(a):
-        relay(a, 0, 0, 1, 0)
-        relay(a, 0, 0, 3, 0)
-        relay(a, 0, 0, 0, 1)
+        for tx, ty in ((1, 0), (3, 0), (0, 1), (1, 1), (3, 1)):
+            relay(a, 0, 0, tx, ty)
         share(a, 0, 0)
-
-    def other_side(a):
-        take(a, 0, 1)
-        relay(a, 0, 1, 1, 0)
-        relay(a, 0, 1, 3, 0)
-        share(a, 0, 1)
 
     def neighbours(a):
         for dy in range(2):
             take(a, 1, dy)
             relay(a, 1, dy, 3, 0)
             share(a, 1, dy)
-        for dy in range(2):
-            take(a, 3, dy)
-            share(a, 3, dy)
+        for dx, dy in ((3, 0), (0, 1), (3, 1)):
+            take(a, dx, dy)
+            share(a, dx, dy)
 
     def opposite(a):
         for dy in range(2):
@@ -207,9 +202,24 @@
                 k = dx * 2 + dy
                 remote(ref, ref, s2.at[a, k], r2.at[a, k], sibling).wait_recv()
 
+    passed_on = [0]
+
+    def pass_ready():
+        k = passed_on[0]
+        if 0 < k <= 7:
+            pl.semaphore_wait(up, 1)
+        if 0 < k <= 3:
+            pl.semaphore_wait(down, 1)
+        if k < 7:
+            pl.semaphore_signal(up, inc=1, device_id=below, device_id_type=MESH)
+        if k < 3:
+            pl.semaphore_signal(down, inc=1, device_id=above, device_id_type=MESH)
+        passed_on[0] += 1
+
     offer(0)
     offer(1)
     own_item(2)
+    pass_ready()
     listed = [order[j] for j in range(NBF)]
 
     def inverse(r, carry):
@@ -232,8 +242,10 @@
     lax.fori_loop(0, TILES, widen, 0)
     sends[...] = jnp.zeros_like(sends)
     collect(0)
-    other_side(2)
+    pass_ready()
     collect(1)
+    pass_ready()
+    neighbours(2)
     from_sibling(0)
     for i in range(DI // CH):
         wfa[:, CH * i : CH * (i + 1)] = gwf[i]
@@ -251,14 +263,14 @@
         return carry
 
     lax.fori_loop(0, 3, convolve, 0)
-    neighbours(2)
-    lax.fori_loop(3, 6, convolve, 0)
+    pass_ready()
+    opposite(2)
     from_sibling(1)
     tsend[...] = gt[order[NBF - 1]]
     sent_tail = push(tsend, trecv, st, rt, ahead)
     sent.append(sent_tail)
-    opposite(2)
-    lax.fori_loop(6, TILES, convolve, 0)
+    lax.fori_loop(3, TILES, convolve, 0)
+    pass_ready()
     rate2[...] = -jnp.exp(wfa[8:WROWS]) * LOG2E
     rearranged = scan_rows()
     load_z.wait()
@@ -270,6 +282,7 @@
         return carry
 
     lax.fori_loop(0, DI // 256, gate, 0)
+    pass_ready()
     from_sibling(2)
     for i in range(DI // CH):
         wba[:, CH * i : CH * (i + 1)] = gwb[i].astype(F32)
@@ -300,6 +313,7 @@
         return carry
 
     lax.fori_loop(0, DI // 256, rearrange, 0)
+    pass_ready()
     proj = lax.dot_general(
         signal[...].astype(BF16),
         wba[DTR:WB].astype(BF16),
@@ -323,6 +337,7 @@
         return carry
 
     lax.fori_loop(0, DI // 256, steps, 0)
+    pass_ready()
     m1 = sub % 4 >= 1
     m2 = sub % 4 >= 2
 
@@ -341,9 +356,10 @@
             rows = rows_of(t)
             now = step[rows, lanes]
             drive = now * signal[rows, lanes]
-            states = tuple(
-                jnp.exp2(now * rates[n]) * states[n] + in_b[n, rows, :] * drive for n in range(NS)
-            )
+            decay = [jnp.exp2(now * rates[n]) for n in range(NS)]
+            for n in range(NS):
+                grown[n, rows, lanes] = decay[n]
+            states = tuple(decay[n] * states[n] + in_b[n, rows, :] * drive for n in range(NS))
             return states, total + now
 
         states, total = lax.fori_loop(0, STEPS, one, ((zero,) * NS, zero), unroll=4)
@@ -398,26 +414,25 @@
         skip = jnp.broadcast_to(wfa[6:7, lanes], full)
 
         def one(t, held):
-            states, total = held
+            states, reached = held
             rows = rows_of(t)
-            now = step[rows, lanes]
             sig = signal[rows, lanes]
-            drive = now * sig
-            total = total + now
-            states = tuple(
-                jnp.exp2(now * rates[n]) * states[n] + in_b[n, rows, :] * drive for n in range(NS)
-            )
+            drive = step[rows, lanes] * sig
+            decay = [grown[n, rows, lanes] for n in range(NS)]
+            states = tuple(decay[n] * states[n] + in_b[n, rows, :] * drive for n in range(NS))
+            reached = tuple(decay[n] * reached[n] for n in range(NS))
             coeffs = [out_b[n, rows, :] for n in range(NS)]
             terms = [coeffs[n] * states[n] for n in range(NS)]
             for n in range(NS):
-                grown[n, rows, lanes] = coeffs[n] * jnp.exp2(total * rates[n])
+                grown[n, rows, lanes] = coeffs[n] * reached[n]
             while len(terms) > 1:
                 terms = [a + b for a, b in zip(terms[::2], terms[1::2])]
             y[rows, lanes] = terms[0] + skip * sig
-            return states, total
+            return states, reached
 
         states = tuple(inner[n, :, lanes] for n in range(NS))
-        lax.fori_loop(0, STEPS, one, (states, reach[:, lanes]), unroll=2)
+        reached = tuple(jnp.exp2(rates[n] * reach[:, lanes]) for n in range(NS))
+        lax.fori_loop(0, STEPS, one, (states, reached), unroll=2)
         return carry
 
     lax.fori_loop(0, 3, own_outputs, 0)
@@ -629,6 +644,7 @@
     scratch = [pltpu.SMEM((NBF,), jnp.int32) if h is None else pltpu.VMEM(*h) for h in held]
     scratch += [dma((2,))] + [dma((3, 8))] * 4 + [dma] * 2
     scratch += [dma((16,))] * 2 + [dma((8,))] * 4 + [dma((16,))] * 4
+    scratch += [pltpu.SemaphoreType.REGULAR] * 2
     gated = pl.pallas_call(
         layer,
         out_shape=jax.ShapeDtypeStruct((TOK, DI), BF16),

time: 72.4 us -> 74.3 us (1.026)
  Pallas kernels: 69.6 us -> 71 us
    pallas_call x1, Pallas kernels: 69.6 us -> 71 us  [shards(): pl.pallas_call(layer, out_shape=jax.ShapeDtypeStruct((TOK, DI), BF16), in...]
where the time goes in v3:
time: 74.3 us; the launch traced here: 73.7 us
  Pallas kernels  71 us (96%)
  matrix products  2.66 us (4%)
    pallas_call x1, Pallas kernels, shards(): pl.pallas_call(layer, out_shape=jax.ShapeDtypeStruct((TOK, DI), BF16), in...  71 us
    dot_general x1, matrix products, shards(): mixed = jnp.dot(gated, out_weight, preferred_element_type=F32).astype(BF16)  2.66 us

profile of v3, /device:TPU:1, one launch (start us, length us, event | category | flops | bytes accessed | tf_op | source)
XLA Modules:
  0.0 73.7 jit_solution(14506986246668010191)
XLA Ops:
  0.0 0.0 copy-start
  0.0 71.0 %layer.1 = bf16[256,1536]{1,0:T(8,128)(2,1)} custom-call(bf16[256,1536]{1,0:T(8,128)(2,1)} %bitcast.9, bf16[256,1536]{1,0:T(8,128)(2,1)} %bitcast.10, f32[4,96]{1,0:T(4,128)} %cw.1, f32[1,96]{1,0:T(1,128)} %bitcast.12, bf16[80,96]{1,0:T(8,128)(2,1)} %bitcast.11, bf16[48,96]{1,0:T(8,128)(2,1)} %sw.1, f32[1,96]{1,0:T(1,128)} %bitcast.13, f32[16,96]{1,0:T(8,128)} %dl.1, ...), custom_call_target="tpu_custom_call" | custom-call | tf_op jit(solution)/shard_map/layer/pallas_call | solution.py:648
  71.0 0.0 copy-done
  71.0 2.7 %convolution_convert_fusion = bf16[256,768]{1,0:T(8,128)(2,1)} fusion(bf16[256,1536]{1,0:T(8,128)(2,1)} %layer.1, bf16[1536,768]{1,0:T(8,128)(2,1)S(1)} %copy-done), kind=kOutput, calls=%fused_computation | convolution fusion | flops 604176384 | bytes 3538944 | tf_op jit(solution)/shard_map/dot_general | solution.py:670
Async XLA Ops:
  0.0 71.0 %copy-start = (bf16[1536,768]{1,0:T(8,128)(2,1)S(1)}, bf16[1536,768]{1,0:T(8,128)(2,1)}, u32[]{:S(2)}) copy-start(bf16[1536,768]{1,0:T(8,128)(2,1)} %param.20) | copy-start | bytes 7077892

commit v4 on v2

--- a/solution.py
+++ b/solution.py
@@ -21,6 +21,8 @@
 STEPS = TOK // CHUNKS
 WROWS = 24
 TROWS = 48
+TAIL = (KC - 1) * TILES
+PAIR = 80
 WB = DTR + DTR + 2 * NS
 SEATS = 8
 VMEM_LIMIT = 56 * 1024 * 1024
@@ -57,7 +59,7 @@
 
 def layer(
     x, z, cw, cb, pwt, sw, sb, dl, sg, order, out,
-    xv, zv, gwf, gwb, gt, tstage, tsend, trecv, where_to,
+    xv, zv, gwf, gwb, gt, tstage, wstage, tsel, tsend, trecv, where_to,
     wfa, wba, xf, sigt, gz, signal, step, rate2, rate_own, in_b, out_b, inner, reach, y, gated, grown,
     sends, recv, scan_e, scan_t, pk1, got1, pk2, got2, bsend, back, fsend, fback,
     local, s1, r1, s2, r2, st, rt, sa, ra, sb1, rb1, sc, rc, sd, rd, sf, rf,
@@ -128,8 +130,12 @@
     gwf[s, 6:7] = sg[...]
     gwf[s, 7:8] = jnp.zeros((1, CH), F32)
     gwf[s, 8:WROWS] = dl[...]
-    gwb[s, 0:DTR] = sw[...]
-    gwb[s, DTR:WB] = pwt[...]
+    narrow = pwt[...].astype(F32)
+    wstage[0:DTR, 0:CH] = sw[...].astype(F32)
+    wstage[DTR:CH, 0:CH] = narrow[0:DTR]
+    for m in range(3):
+        wstage[32 * m : 32 * (m + 1), CH:LANES] = narrow[DTR:, 32 * m : 32 * (m + 1)]
+    gwb[s] = wstage[...].astype(BF16)
     tstage[...] = jnp.zeros_like(tstage)
     load_x.wait()
     for b in range(2):
@@ -137,12 +143,13 @@
         for t in range(KC - 1):
             for j in range(TILES):
                 line = ends[13 + t : 14 + t, LANES * j : LANES * (j + 1)]
-                tstage[b, t * TILES + j : t * TILES + j + 1] = line
-    gt[pl.ds(2 * s, 2)] = tstage[...].astype(BF16)
+                at = b * TAIL + t * TILES + j
+                tstage[at : at + 1] = line
+    gt[s] = tstage[...].astype(BF16)
     pl.semaphore_wait(barrier, width + SEATS + outer + 2)
 
     def place(a, i):
-        return (gwf.at[i], gt.at[pl.ds(2 * i, 2)], gwb.at[i])[a]
+        return (gwf.at[i], gt.at[i], gwb.at[i])[a]
 
     sent = []
     relayed = [0, 0, 0]
@@ -155,6 +162,11 @@
         frame = twin if ty and a != 1 else f
         sent.append(push(ref, ref, ssem, r1.at[a, landing], (frame, chip(tx, ty))))
 
+    def tail_of(block):
+        pair = gt[lax.shift_right_logical(block, 1)].astype(F32)
+        odd = jnp.full((TAIL, LANES), block & 1, jnp.int32) == 1
+        return jnp.where(odd, pair[TAIL : 2 * TAIL], pair[0:TAIL])
+
     def share(a, dx, dy):
         ref = place(a, chip(dx, dy))
         k = dx * 2 + dy
@@ -164,26 +176,22 @@
         ref = place(a, chip(dx, dy))
         remote(ref, ref, s1.at[a, 0], r1.at[a, dx * 2 + dy], sibling).wait_recv()
 
-    def offer(a):
-        for tx, ty in ((1, 0), (3, 0), (0, 1), (1, 1), (3, 1), (2, 0), (2, 1)):
+    def offer(a, targets):
+        for tx, ty in targets:
             relay(a, 0, 0, tx, ty)
         share(a, 0, 0)
 
-    def collect(a):
-        for dx, dy in ((3, 0), (1, 0), (0, 1), (3, 1), (1, 1), (2, 0), (2, 1)):
+    def collect(a, items):
+        for dx, dy in items:
             take(a, dx, dy)
             share(a, dx, dy)
-
-    def own_item(a):
-        relay(a, 0, 0, 1, 0)
-        relay(a, 0, 0, 3, 0)
-        relay(a, 0, 0, 0, 1)
-        share(a, 0, 0)
 
     def other_side(a):
         take(a, 0, 1)
         relay(a, 0, 1, 1, 0)
         relay(a, 0, 1, 3, 0)
+        if a == 1:
+            relay(a, 0, 1, 2, 0)
         share(a, 0, 1)
 
     def neighbours(a):
@@ -207,9 +215,9 @@
                 k = dx * 2 + dy
                 remote(ref, ref, s2.at[a, k], r2.at[a, k], sibling).wait_recv()
 
-    offer(0)
-    offer(1)
-    own_item(2)
+    offer(0, ((0, 1), (1, 1), (3, 1), (2, 1), (1, 0), (3, 0), (2, 0)))
+    offer(1, ((0, 1), (2, 0), (1, 0), (3, 0)))
+    offer(2, ((0, 1), (1, 0), (3, 0)))
     listed = [order[j] for j in range(NBF)]
 
     def inverse(r, carry):
@@ -231,9 +239,10 @@
 
     lax.fori_loop(0, TILES, widen, 0)
     sends[...] = jnp.zeros_like(sends)
-    collect(0)
+    other_side(1)
     other_side(2)
-    collect(1)
+    collect(0, ((3, 0), (1, 0), (0, 1), (3, 1), (1, 1), (2, 0), (2, 1)))
+    collect(1, ((1, 0), (3, 0), (2, 0), (1, 1), (3, 1), (2, 1)))
     from_sibling(0)
     for i in range(DI // CH):
         wfa[:, CH * i : CH * (i + 1)] = gwf[i]
@@ -254,7 +263,9 @@
     neighbours(2)
     lax.fori_loop(3, 6, convolve, 0)
     from_sibling(1)
-    tsend[...] = gt[order[NBF - 1]]
+    tsel[...] = jnp.zeros_like(tsel)
+    tsel[0:TAIL] = tail_of(order[NBF - 1])
+    tsend[...] = tsel[...].astype(BF16)
     sent_tail = push(tsend, trecv, st, rt, ahead)
     sent.append(sent_tail)
     opposite(2)
@@ -272,15 +283,18 @@
     lax.fori_loop(0, DI // 256, gate, 0)
     from_sibling(2)
     for i in range(DI // CH):
-        wba[:, CH * i : CH * (i + 1)] = gwb[i].astype(F32)
+        held = gwb[i].astype(F32)
+        wba[0:CH, CH * i : CH * (i + 1)] = held[:, 0:CH]
+        for m in range(3):
+            at = CH * i + 32 * m
+            wba[CH:WB, at : at + 32] = held[32 * m : 32 * (m + 1), CH:LANES]
     sent_tail.wait_recv()
-    came = trecv[...].astype(F32)
-    opening = jnp.full(came.shape, f, jnp.int32) == 0
-    gt[NBF] = jnp.where(opening, 0.0, came).astype(BF16)
+    came = trecv[...].astype(F32)[0:TAIL]
+    came = jnp.where(jnp.full(came.shape, f, jnp.int32) == 0, 0.0, came)
     for b in range(2):
         at = where_to[2 * s + b]
-        before = jnp.where(at == 0, NBF, order[jnp.maximum(at - 1, 0)])
-        halo = gt[before].astype(F32)
+        found = tail_of(order[jnp.maximum(at - 1, 0)])
+        halo = jnp.where(jnp.full(came.shape, at, jnp.int32) == 0, came, found)
         for t in range(KC - 1):
             for j in range(TILES):
                 line = halo[t * TILES + j : t * TILES + j + 1]
@@ -309,15 +323,12 @@
     spread_columns(proj, DTR, in_b)
     rank = proj[:, :DTR]
     high = rank.astype(BF16)
-    rest = rank - high.astype(F32)
-    mid = rest.astype(BF16)
-    low = (rest - mid.astype(F32)).astype(BF16)
+    low = (rank - high.astype(F32)).astype(BF16)
 
     def steps(chunk, carry):
         lanes = lanes_of(chunk, 256)
         weight = wba[0:DTR, lanes].astype(BF16)
         total = wfa[5:6, lanes] + jnp.dot(low, weight, preferred_element_type=F32)
-        total = total + jnp.dot(mid, weight, preferred_element_type=F32)
         total = total + jnp.dot(high, weight, preferred_element_type=F32)
         step[:, lanes] = jnp.maximum(total, 0.0) + jnp.log1p(jnp.exp(-jnp.abs(total)))
         return carry
@@ -469,6 +480,8 @@
         peer = (s + d) % width
         returns.append(push(bsend.at[peer], back.at[s], sd.at[peer], rd.at[s], (f, peer)))
     lax.fori_loop(3, 6, own_outputs, 0)
+    for copy in sent[: len(sent) // 2]:
+        copy.wait_send()
     for copy in level1:
         copy.wait_recv()
 
@@ -489,6 +502,8 @@
     for d in range(1, outer):
         level2.append(push(pk2, got2.at[part], sc.at[d], rc.at[d], (far(d), s)))
     lax.fori_loop(6, 9, own_outputs, 0)
+    for copy in sent[len(sent) // 2 :] + level1:
+        copy.wait_send()
     for copy in level2:
         copy.wait_recv()
 
@@ -508,6 +523,10 @@
         peer = (s + d) % width
         starts.append(push(fsend, fback.at[s], sf.at[peer], rf.at[s], (f, peer)))
     lax.fori_loop(9, 12, own_outputs, 0)
+    for copy in level2 + returns:
+        copy.wait_send()
+    for d in range(1, width):
+        to_owner((s + d) % width).wait_send()
     for d in range(1, width):
         peer = (s + d) % width
         remote(bsend.at[peer], back.at[peer], sd.at[peer], rd.at[peer], (f, peer)).wait_recv()
@@ -561,10 +580,8 @@
         return carry
 
     lax.fori_loop(0, 4, one_group_back, 0)
-    for copy in sent + level1 + level2 + returns + starts:
+    for copy in starts:
         copy.wait_send()
-    for d in range(1, width):
-        to_owner((s + d) % width).wait_send()
 
 
 def shards(
@@ -591,9 +608,11 @@
         ((TOK, DI), BF16),
         ((TOK, DI), BF16),
         ((space, WROWS, CH), F32),
-        ((space, WB, CH), BF16),
-        ((NBF + 1, TROWS, LANES), BF16),
-        ((2, TROWS, LANES), F32),
+        ((space, CH, LANES), BF16),
+        ((space, PAIR, LANES), BF16),
+        ((PAIR, LANES), F32),
+        ((CH, LANES), F32),
+        ((TROWS, LANES), F32),
         ((TROWS, LANES), BF16),
         ((TROWS, LANES), BF16),
         None,

time: 72.4 us -> 70.6 us (0.975)
  Pallas kernels: 69.6 us -> 67.7 us
    pallas_call x1, Pallas kernels: 69.6 us -> 67.7 us  [shards(): pl.pallas_call(layer, out_shape=jax.ShapeDtypeStruct((TOK, DI), BF16), in...]
where the time goes in v4:
time: 70.6 us; the launch traced here: 70.4 us
  Pallas kernels  67.7 us (96%)
  matrix products  2.66 us (4%)
    pallas_call x1, Pallas kernels, shards(): pl.pallas_call(layer, out_shape=jax.ShapeDtypeStruct((TOK, DI), BF16), in...  67.7 us
    dot_general x1, matrix products, shards(): mixed = jnp.dot(gated, out_weight, preferred_element_type=F32).astype(BF16)  2.66 us

profile of v4, /device:TPU:1, one launch (start us, length us, event | category | flops | bytes accessed | tf_op | source)
XLA Modules:
  0.0 70.4 jit_solution(11453432556978604424)
XLA Ops:
  0.0 0.0 copy-start
  0.0 67.7 %layer.1 = bf16[256,1536]{1,0:T(8,128)(2,1)} custom-call(bf16[256,1536]{1,0:T(8,128)(2,1)} %bitcast.9, bf16[256,1536]{1,0:T(8,128)(2,1)} %bitcast.10, f32[4,96]{1,0:T(4,128)} %cw.1, f32[1,96]{1,0:T(1,128)} %bitcast.12, bf16[80,96]{1,0:T(8,128)(2,1)} %bitcast.11, bf16[48,96]{1,0:T(8,128)(2,1)} %sw.1, f32[1,96]{1,0:T(1,128)} %bitcast.13, f32[16,96]{1,0:T(8,128)} %dl.1, ...), custom_call_target="tpu_custom_call" | custom-call | tf_op jit(solution)/shard_map/layer/pallas_call | solution.py:651
  67.8 0.0 copy-done
  67.8 2.7 %convolution_convert_fusion = bf16[256,768]{1,0:T(8,128)(2,1)} fusion(bf16[256,1536]{1,0:T(8,128)(2,1)} %layer.1, bf16[1536,768]{1,0:T(8,128)(2,1)S(1)} %copy-done), kind=kOutput, calls=%fused_computation | convolution fusion | flops 604176384 | bytes 3538944 | tf_op jit(solution)/shard_map/dot_general | solution.py:673
Async XLA Ops:
  0.0 67.8 %copy-start = (bf16[1536,768]{1,0:T(8,128)(2,1)S(1)}, bf16[1536,768]{1,0:T(8,128)(2,1)}, u32[]{:S(2)}) copy-start(bf16[1536,768]{1,0:T(8,128)(2,1)} %param.20) | copy-start | bytes 7077892

commit v5 on v4

--- a/solution.py
+++ b/solution.py
@@ -62,7 +62,7 @@
     xv, zv, gwf, gwb, gt, tstage, wstage, tsel, tsend, trecv, where_to,
     wfa, wba, xf, sigt, gz, signal, step, rate2, rate_own, in_b, out_b, inner, reach, y, gated, grown,
     sends, recv, scan_e, scan_t, pk1, got1, pk2, got2, bsend, back, fsend, fback,
-    local, s1, r1, s2, r2, st, rt, sa, ra, sb1, rb1, sc, rc, sd, rd, sf, rf,
+    local, s1, r1, s2, r2, st, rt, sa, ra, sb1, rb1, sc, rc, sd, rd, sf, rf, up, down,
 ):
     f = lax.axis_index("tm")
     s = lax.axis_index("space")
@@ -117,8 +117,10 @@
         pl.semaphore_signal(barrier, inc=1, device_id=(f, (s + d) % width), device_id_type=MESH)
     for d in range(1, SEATS):
         pl.semaphore_signal(barrier, inc=1, device_id=(near(d), s), device_id_type=MESH)
-    for d in range(1, outer):
-        pl.semaphore_signal(barrier, inc=1, device_id=(far(d), s), device_id_type=MESH)
+    above = ((f + 2) % frames, s)
+    below = ((f + frames - 2) % frames, s)
+    for neighbour in (above, below):
+        pl.semaphore_signal(barrier, inc=1, device_id=neighbour, device_id_type=MESH)
     pl.semaphore_signal(barrier, inc=1, device_id=behind, device_id_type=MESH)
     for dx in range(4):
         pl.semaphore_signal(barrier, inc=1, device_id=(twin, chip(dx, 1)), device_id_type=MESH)
@@ -137,6 +139,76 @@
         wstage[32 * m : 32 * (m + 1), CH:LANES] = narrow[DTR:, 32 * m : 32 * (m + 1)]
     gwb[s] = wstage[...].astype(BF16)
     tstage[...] = jnp.zeros_like(tstage)
+    pl.semaphore_wait(barrier, width + SEATS + 5)
+
+    def place(a, i):
+        return (gwf.at[i], gt.at[i], gwb.at[i])[a]
+
+    sent = []
+    relayed = [0, 0, 0]
+
+    def relay(a, dx, dy, tx, ty):
+        ref = place(a, chip(dx, dy))
+        landing = (dx - tx) % 4 * 2 + (dy - ty) % 2
+        ssem = s1.at[a, relayed[a]]
+        relayed[a] += 1
+        frame = twin if ty and a != 1 else f
+        sent.append(push(ref, ref, ssem, r1.at[a, landing], (frame, chip(tx, ty))))
+
+    def tail_of(block):
+        pair = gt[lax.shift_right_logical(block, 1)].astype(F32)
+        odd = jnp.full((TAIL, LANES), block & 1, jnp.int32) == 1
+        return jnp.where(odd, pair[TAIL : 2 * TAIL], pair[0:TAIL])
+
+    def share(a, dx, dy):
+        ref = place(a, chip(dx, dy))
+        k = dx * 2 + dy
+        sent.append(push(ref, ref, s2.at[a, k], r2.at[a, k], sibling))
+
+    def take(a, dx, dy):
+        ref = place(a, chip(dx, dy))
+        remote(ref, ref, s1.at[a, 0], r1.at[a, dx * 2 + dy], sibling).wait_recv()
+
+    def offer(a, targets):
+        for tx, ty in targets:
+            relay(a, 0, 0, tx, ty)
+        share(a, 0, 0)
+
+    def collect(a, items):
+        for dx, dy in items:
+            take(a, dx, dy)
+            share(a, dx, dy)
+
+    def other_side(a):
+        take(a, 0, 1)
+        relay(a, 0, 1, 1, 0)
+        relay(a, 0, 1, 3, 0)
+        if a == 1:
+            relay(a, 0, 1, 2, 0)
+        share(a, 0, 1)
+
+    def neighbours(a):
+        for dy in range(2):
+            take(a, 1, dy)
+            relay(a, 1, dy, 3, 0)
+            share(a, 1, dy)
+        for dy in range(2):
+            take(a, 3, dy)
+            share(a, 3, dy)
+
+    def opposite(a):
+        for dy in range(2):
+            take(a, 2, dy)
+            share(a, 2, dy)
+
+    def from_sibling(a):
+        for dx in range(4):
+            for dy in range(2):
+                ref = place(a, chip(dx, dy) - core + 1 - core)
+                k = dx * 2 + dy
+                remote(ref, ref, s2.at[a, k], r2.at[a, k], sibling).wait_recv()
+
+    offer(0, ((0, 1), (1, 1), (3, 1), (2, 1), (1, 0), (3, 0), (2, 0)))
     load_x.wait()
     for b in range(2):
         ends = xv[BLK * (b + 1) - 16 : BLK * (b + 1)].astype(F32)
@@ -146,78 +218,23 @@
                 at = b * TAIL + t * TILES + j
                 tstage[at : at + 1] = line
     gt[s] = tstage[...].astype(BF16)
-    pl.semaphore_wait(barrier, width + SEATS + outer + 2)
-
-    def place(a, i):
-        return (gwf.at[i], gt.at[i], gwb.at[i])[a]
-
-    sent = []
-    relayed = [0, 0, 0]
-
-    def relay(a, dx, dy, tx, ty):
-        ref = place(a, chip(dx, dy))
-        landing = (dx - tx) % 4 * 2 + (dy - ty) % 2
-        ssem = s1.at[a, relayed[a]]
-        relayed[a] += 1
-        frame = twin if ty and a != 1 else f
-        sent.append(push(ref, ref, ssem, r1.at[a, landing], (frame, chip(tx, ty))))
-
-    def tail_of(block):
-        pair = gt[lax.shift_right_logical(block, 1)].astype(F32)
-        odd = jnp.full((TAIL, LANES), block & 1, jnp.int32) == 1
-        return jnp.where(odd, pair[TAIL : 2 * TAIL], pair[0:TAIL])
-
-    def share(a, dx, dy):
-        ref = place(a, chip(dx, dy))
-        k = dx * 2 + dy
-        sent.append(push(ref, ref, s2.at[a, k], r2.at[a, k], sibling))
-
-    def take(a, dx, dy):
-        ref = place(a, chip(dx, dy))
-        remote(ref, ref, s1.at[a, 0], r1.at[a, dx * 2 + dy], sibling).wait_recv()
-
-    def offer(a, targets):
-        for tx, ty in targets:
-            relay(a, 0, 0, tx, ty)
-        share(a, 0, 0)
-
-    def collect(a, items):
-        for dx, dy in items:
-            take(a, dx, dy)
-            share(a, dx, dy)
-
-    def other_side(a):
-        take(a, 0, 1)
-        relay(a, 0, 1, 1, 0)
-        relay(a, 0, 1, 3, 0)
-        if a == 1:
-            relay(a, 0, 1, 2, 0)
-        share(a, 0, 1)
-
-    def neighbours(a):
-        for dy in range(2):
-            take(a, 1, dy)
-            relay(a, 1, dy, 3, 0)
-            share(a, 1, dy)
-        for dy in range(2):
-            take(a, 3, dy)
-            share(a, 3, dy)
-
-    def opposite(a):
-        for dy in range(2):
-            take(a, 2, dy)
-            share(a, 2, dy)
-
-    def from_sibling(a):
-        for dx in range(4):
-            for dy in range(2):
-                ref = place(a, chip(dx, dy) - core + 1 - core)
-                k = dx * 2 + dy
-                remote(ref, ref, s2.at[a, k], r2.at[a, k], sibling).wait_recv()
-
-    offer(0, ((0, 1), (1, 1), (3, 1), (2, 1), (1, 0), (3, 0), (2, 0)))
     offer(1, ((0, 1), (2, 0), (1, 0), (3, 0)))
     offer(2, ((0, 1), (1, 0), (3, 0)))
+    passed_on = [0]
+
+    def pass_ready():
+        k = passed_on[0]
+        if 0 < k <= 7:
+            pl.semaphore_wait(up, 1)
+        if 0 < k <= 3:
+            pl.semaphore_wait(down, 1)
+        if k < 7:
+            pl.semaphore_signal(up, inc=1, device_id=below, device_id_type=MESH)
+        if k < 3:
+            pl.semaphore_signal(down, inc=1, device_id=above, device_id_type=MESH)
+        passed_on[0] += 1
+
+    pass_ready()
     listed = [order[j] for j in range(NBF)]
 
     def inverse(r, carry):
@@ -241,8 +258,10 @@
     sends[...] = jnp.zeros_like(sends)
     other_side(1)
     other_side(2)
+    pass_ready()
     collect(0, ((3, 0), (1, 0), (0, 1), (3, 1), (1, 1), (2, 0), (2, 1)))
     collect(1, ((1, 0), (3, 0), (2, 0), (1, 1), (3, 1), (2, 1)))
+    pass_ready()
     from_sibling(0)
     for i in range(DI // CH):
         wfa[:, CH * i : CH * (i + 1)] = gwf[i]
@@ -260,6 +279,7 @@
         return carry
 
     lax.fori_loop(0, 3, convolve, 0)
+    pass_ready()
     neighbours(2)
     lax.fori_loop(3, 6, convolve, 0)
     from_sibling(1)
@@ -270,6 +290,7 @@
     sent.append(sent_tail)
     opposite(2)
     lax.fori_loop(6, TILES, convolve, 0)
+    pass_ready()
     rate2[...] = -jnp.exp(wfa[8:WROWS]) * LOG2E
     rearranged = scan_rows()
     load_z.wait()
@@ -281,6 +302,7 @@
         return carry
 
     lax.fori_loop(0, DI // 256, gate, 0)
+    pass_ready()
     from_sibling(2)
     for i in range(DI // CH):
         held = gwb[i].astype(F32)
@@ -314,6 +336,7 @@
         return carry
 
     lax.fori_loop(0, DI // 256, rearrange, 0)
+    pass_ready()
     proj = lax.dot_general(
         signal[...].astype(BF16),
         wba[DTR:WB].astype(BF16),
@@ -334,6 +357,7 @@
         return carry
 
     lax.fori_loop(0, DI // 256, steps, 0)
+    pass_ready()
     m1 = sub % 4 >= 1
     m2 = sub % 4 >= 2
 
@@ -380,8 +404,9 @@
                 moved = pltpu.roll(two_s, turn, 0) if turn else two_s
                 state_out = jnp.where(sub % 4 == q, moved, state_out)
                 rate_out = jnp.where(sub % 4 == q, rates[n], rate_out)
-            sends[group * 4 + h, place] = state_out
-            sends[group * 4 + h, 3] = jnp.where(sub % 4 == place, ends, sends[group * 4 + h, 3])
+            owner = h * 4 + group
+            sends[owner, place] = state_out
+            sends[owner, 3] = jnp.where(sub % 4 == place, ends, sends[owner, 3])
             rate_own[h, tile] = rate_out
         return carry
 
@@ -391,7 +416,7 @@
     def one_group(g, carry):
         lax.fori_loop(g * 3, g * 3 + 3, block_states, 0)
         for h in range(4):
-            peer = g * 4 + h
+            peer = h * 4 + g
 
             @pl.when(peer != s)
             def _():
@@ -439,8 +464,8 @@
     def turned(v):
         return pltpu.roll(v, 4, len(v.shape) - 2)
 
-    my_group = s // 4
-    my_rates = rate_own[s % 4, pl.ds(my_group * 3, 3)]
+    my_group = s % 4
+    my_rates = rate_own[s // 4, pl.ds(my_group * 3, 3)]
 
     def decays(sums):
         spread = [jnp.broadcast_to(sums[i : i + 1], full) for i in range(3)]
@@ -474,11 +499,6 @@
         return carry
 
     lax.fori_loop(0, width, pack, 0, unroll=4)
-    back[s] = bsend[s]
-    returns = []
-    for d in range(1, width):
-        peer = (s + d) % width
-        returns.append(push(bsend.at[peer], back.at[s], sd.at[peer], rd.at[s], (f, peer)))
     lax.fori_loop(3, 6, own_outputs, 0)
     for copy in sent[: len(sent) // 2]:
         copy.wait_send()
@@ -501,6 +521,11 @@
     level2 = []
     for d in range(1, outer):
         level2.append(push(pk2, got2.at[part], sc.at[d], rc.at[d], (far(d), s)))
+    back[s] = bsend[s]
+    returns = []
+    for d in range(1, width):
+        peer = (s + d) % width
+        returns.append(push(bsend.at[peer], back.at[s], sd.at[peer], rd.at[s], (f, peer)))
     lax.fori_loop(6, 9, own_outputs, 0)
     for copy in sent[len(sent) // 2 :] + level1:
         copy.wait_send()
@@ -541,11 +566,11 @@
     def complete(g, place):
         lanes = lanes_of(g * 3 + place)
         rates = rates_of(lanes)
-        passed = both(back[g * 4, 3], place)
+        passed = both(back[g, 3], place)
         entering = []
         for h in range(4):
-            came = back[g * 4 + h, place]
-            begun = fback[g * 4 + h].astype(F32)
+            came = back[h * 4 + g, place]
+            begun = fback[h * 4 + g].astype(F32)
             for q in range(4):
                 r = place * 4 + q
                 line = jnp.broadcast_to(begun[r : r + 1], full)
@@ -567,7 +592,7 @@
 
     def one_group_back(g, carry):
         for h in range(4):
-            peer = g * 4 + h
+            peer = h * 4 + g
 
             @pl.when(peer != s)
             def _():
@@ -648,6 +673,7 @@
     scratch = [pltpu.SMEM((NBF,), jnp.int32) if h is None else pltpu.VMEM(*h) for h in held]
     scratch += [dma((2,))] + [dma((3, 8))] * 4 + [dma] * 2
     scratch += [dma((16,))] * 2 + [dma((8,))] * 4 + [dma((16,))] * 4
+    scratch += [pltpu.SemaphoreType.REGULAR] * 2
     gated = pl.pallas_call(
         layer,
         out_shape=jax.ShapeDtypeStruct((TOK, DI), BF16),

time: 70.6 us -> 72.4 us (1.025)
  Pallas kernels: 67.7 us -> 69.5 us
    pallas_call x1, Pallas kernels: 67.7 us -> 69.5 us  [shards(): pl.pallas_call(layer, out_shape=jax.ShapeDtypeStruct((TOK, DI), BF16), in...]
where the time goes in v5:
time: 72.4 us; the launch traced here: 72.2 us
  Pallas kernels  69.5 us (96%)
  matrix products  2.66 us (4%)
    pallas_call x1, Pallas kernels, shards(): pl.pallas_call(layer, out_shape=jax.ShapeDtypeStruct((TOK, DI), BF16), in...  69.5 us
    dot_general x1, matrix products, shards(): mixed = jnp.dot(gated, out_weight, preferred_element_type=F32).astype(BF16)  2.66 us

profile of v5, /device:TPU:1, one launch (start us, length us, event | category | flops | bytes accessed | tf_op | source)
XLA Modules:
  0.0 72.2 jit_solution(8181731793032399168)
XLA Ops:
  0.0 0.0 copy-start
  0.0 69.5 %layer.1 = bf16[256,1536]{1,0:T(8,128)(2,1)} custom-call(bf16[256,1536]{1,0:T(8,128)(2,1)} %bitcast.9, bf16[256,1536]{1,0:T(8,128)(2,1)} %bitcast.10, f32[4,96]{1,0:T(4,128)} %cw.1, f32[1,96]{1,0:T(1,128)} %bitcast.12, bf16[80,96]{1,0:T(8,128)(2,1)} %bitcast.11, bf16[48,96]{1,0:T(8,128)(2,1)} %sw.1, f32[1,96]{1,0:T(1,128)} %bitcast.13, f32[16,96]{1,0:T(8,128)} %dl.1, ...), custom_call_target="tpu_custom_call" | custom-call | tf_op jit(solution)/shard_map/layer/pallas_call | solution.py:677
  69.5 0.0 copy-done
  69.5 2.7 %convolution_convert_fusion = bf16[256,768]{1,0:T(8,128)(2,1)} fusion(bf16[256,1536]{1,0:T(8,128)(2,1)} %layer.1, bf16[1536,768]{1,0:T(8,128)(2,1)S(1)} %copy-done), kind=kOutput, calls=%fused_computation | convolution fusion | flops 604176384 | bytes 3538944 | tf_op jit(solution)/shard_map/dot_general | solution.py:699
Async XLA Ops:
  0.0 69.5 %copy-start = (bf16[1536,768]{1,0:T(8,128)(2,1)S(1)}, bf16[1536,768]{1,0:T(8,128)(2,1)}, u32[]{:S(2)}) copy-start(bf16[1536,768]{1,0:T(8,128)(2,1)} %param.20) | copy-start | bytes 7077892

commit v6 on v5

--- a/solution.py
+++ b/solution.py
@@ -62,7 +62,7 @@
     xv, zv, gwf, gwb, gt, tstage, wstage, tsel, tsend, trecv, where_to,
     wfa, wba, xf, sigt, gz, signal, step, rate2, rate_own, in_b, out_b, inner, reach, y, gated, grown,
     sends, recv, scan_e, scan_t, pk1, got1, pk2, got2, bsend, back, fsend, fback,
-    local, s1, r1, s2, r2, st, rt, sa, ra, sb1, rb1, sc, rc, sd, rd, sf, rf, up, down,
+    local, s1, r1, s2, r2, st, rt, sa, ra, sb1, rb1, sc, rc, sd, rd, sf, rf,
 ):
     f = lax.axis_index("tm")
     s = lax.axis_index("space")
@@ -117,10 +117,8 @@
         pl.semaphore_signal(barrier, inc=1, device_id=(f, (s + d) % width), device_id_type=MESH)
     for d in range(1, SEATS):
         pl.semaphore_signal(barrier, inc=1, device_id=(near(d), s), device_id_type=MESH)
-    above = ((f + 2) % frames, s)
-    below = ((f + frames - 2) % frames, s)
-    for neighbour in (above, below):
-        pl.semaphore_signal(barrier, inc=1, device_id=neighbour, device_id_type=MESH)
+    for d in range(1, outer):
+        pl.semaphore_signal(barrier, inc=1, device_id=(far(d), s), device_id_type=MESH)
     pl.semaphore_signal(barrier, inc=1, device_id=behind, device_id_type=MESH)
     for dx in range(4):
         pl.semaphore_signal(barrier, inc=1, device_id=(twin, chip(dx, 1)), device_id_type=MESH)
@@ -139,7 +137,7 @@
         wstage[32 * m : 32 * (m + 1), CH:LANES] = narrow[DTR:, 32 * m : 32 * (m + 1)]
     gwb[s] = wstage[...].astype(BF16)
     tstage[...] = jnp.zeros_like(tstage)
-    pl.semaphore_wait(barrier, width + SEATS + 5)
+    pl.semaphore_wait(barrier, width + SEATS + outer + 2)
 
     def place(a, i):
         return (gwf.at[i], gt.at[i], gwb.at[i])[a]
@@ -220,21 +218,6 @@
     gt[s] = tstage[...].astype(BF16)
     offer(1, ((0, 1), (2, 0), (1, 0), (3, 0)))
     offer(2, ((0, 1), (1, 0), (3, 0)))
-    passed_on = [0]
-
-    def pass_ready():
-        k = passed_on[0]
-        if 0 < k <= 7:
-            pl.semaphore_wait(up, 1)
-        if 0 < k <= 3:
-            pl.semaphore_wait(down, 1)
-        if k < 7:
-            pl.semaphore_signal(up, inc=1, device_id=below, device_id_type=MESH)
-        if k < 3:
-            pl.semaphore_signal(down, inc=1, device_id=above, device_id_type=MESH)
-        passed_on[0] += 1
-
-    pass_ready()
     listed = [order[j] for j in range(NBF)]
 
     def inverse(r, carry):
@@ -258,10 +241,8 @@
     sends[...] = jnp.zeros_like(sends)
     other_side(1)
     other_side(2)
-    pass_ready()
     collect(0, ((3, 0), (1, 0), (0, 1), (3, 1), (1, 1), (2, 0), (2, 1)))
     collect(1, ((1, 0), (3, 0), (2, 0), (1, 1), (3, 1), (2, 1)))
-    pass_ready()
     from_sibling(0)
     for i in range(DI // CH):
         wfa[:, CH * i : CH * (i + 1)] = gwf[i]
@@ -279,7 +260,6 @@
         return carry
 
     lax.fori_loop(0, 3, convolve, 0)
-    pass_ready()
     neighbours(2)
     lax.fori_loop(3, 6, convolve, 0)
     from_sibling(1)
@@ -290,7 +270,6 @@
     sent.append(sent_tail)
     opposite(2)
     lax.fori_loop(6, TILES, convolve, 0)
-    pass_ready()
     rate2[...] = -jnp.exp(wfa[8:WROWS]) * LOG2E
     rearranged = scan_rows()
     load_z.wait()
@@ -302,7 +281,6 @@
         return carry
 
     lax.fori_loop(0, DI // 256, gate, 0)
-    pass_ready()
     from_sibling(2)
     for i in range(DI // CH):
         held = gwb[i].astype(F32)
@@ -336,7 +314,6 @@
         return carry
 
     lax.fori_loop(0, DI // 256, rearrange, 0)
-    pass_ready()
     proj = lax.dot_general(
         signal[...].astype(BF16),
         wba[DTR:WB].astype(BF16),
@@ -357,7 +334,6 @@
         return carry
 
     lax.fori_loop(0, DI // 256, steps, 0)
-    pass_ready()
     m1 = sub % 4 >= 1
     m2 = sub % 4 >= 2
 
@@ -673,7 +649,6 @@
     scratch = [pltpu.SMEM((NBF,), jnp.int32) if h is None else pltpu.VMEM(*h) for h in held]
     scratch += [dma((2,))] + [dma((3, 8))] * 4 + [dma] * 2
     scratch += [dma((16,))] * 2 + [dma((8,))] * 4 + [dma((16,))] * 4
-    scratch += [pltpu.SemaphoreType.REGULAR] * 2
     gated = pl.pallas_call(
         layer,
         out_shape=jax.ShapeDtypeStruct((TOK, DI), BF16),

time: 72.4 us -> 70.9 us (0.979)
  Pallas kernels: 69.5 us -> 68 us
    pallas_call x1, Pallas kernels: 69.5 us -> 68 us  [shards(): pl.pallas_call(layer, out_shape=jax.ShapeDtypeStruct((TOK, DI), BF16), in...]
where the time goes in v6:
time: 70.9 us; the launch traced here: 70.7 us
  Pallas kernels  68 us (96%)
  matrix products  2.66 us (4%)
    pallas_call x1, Pallas kernels, shards(): pl.pallas_call(layer, out_shape=jax.ShapeDtypeStruct((TOK, DI), BF16), in...  68 us
    dot_general x1, matrix products, shards(): mixed = jnp.dot(gated, out_weight, preferred_element_type=F32).astype(BF16)  2.66 us

profile of v6, /device:TPU:1, one launch (start us, length us, event | category | flops | bytes accessed | tf_op | source)
XLA Modules:
  0.0 70.7 jit_solution(4247059804689481381)
XLA Ops:
  0.0 0.0 copy-start
  0.0 68.0 %layer.1 = bf16[256,1536]{1,0:T(8,128)(2,1)} custom-call(bf16[256,1536]{1,0:T(8,128)(2,1)} %bitcast.9, bf16[256,1536]{1,0:T(8,128)(2,1)} %bitcast.10, f32[4,96]{1,0:T(4,128)} %cw.1, f32[1,96]{1,0:T(1,128)} %bitcast.12, bf16[80,96]{1,0:T(8,128)(2,1)} %bitcast.11, bf16[48,96]{1,0:T(8,128)(2,1)} %sw.1, f32[1,96]{1,0:T(1,128)} %bitcast.13, f32[16,96]{1,0:T(8,128)} %dl.1, ...), custom_call_target="tpu_custom_call" | custom-call | tf_op jit(solution)/shard_map/layer/pallas_call | solution.py:652
  68.1 0.0 copy-done
  68.1 2.7 %convolution_convert_fusion = bf16[256,768]{1,0:T(8,128)(2,1)} fusion(bf16[256,1536]{1,0:T(8,128)(2,1)} %layer.1, bf16[1536,768]{1,0:T(8,128)(2,1)S(1)} %copy-done), kind=kOutput, calls=%fused_computation | convolution fusion | flops 604176384 | bytes 3538944 | tf_op jit(solution)/shard_map/dot_general | solution.py:674
Async XLA Ops:
  0.0 68.1 %copy-start = (bf16[1536,768]{1,0:T(8,128)(2,1)S(1)}, bf16[1536,768]{1,0:T(8,128)(2,1)}, u32[]{:S(2)}) copy-start(bf16[1536,768]{1,0:T(8,128)(2,1)} %param.20) | copy-start | bytes 7077892
